TPU v7x, 256 devices: a whole 4x4x8 slice. The times are simulated.
256 devices in a mesh: sub: 32 (over y, x, core), row: 8 (over z).
Axes of the slice: x: 4, y: 4, z: 8, core: 2. Of those that a mesh axis runs over, the one named last changes fastest.
Arguments:
- source: bfloat16 [4, 32, 4096, 256], P(None, 'sub', 'row'), may hold values from -6 to 6
- inverse_z: bfloat16 [32, 4096, 4096], P('sub', 'row'), may hold values from -1 to 2
- pattern: int32 [32, 16, 16], P('sub', 'row'), may hold values from 0 to 1, as said below
- line_far: int32 [32, 1024, 2], P('sub', 'row'), may hold values from 0 to 1023, as said below
- delay: int32 [32, 1024], P('sub', 'row'), may hold values from 1 to 2, as said below
- xf_node: int32 [32, 64], P('sub', 'row'), may hold values from 0 to 4095, as said below
- wave0: bfloat16 [2, 32, 1024, 256], P(None, 'sub', 'row'), may hold values from -6 to 6
- flux0: float32 [32, 64, 256], P('sub', 'row'), may hold values from -6 to 6
- volt0: float32 [32, 64, 256], P('sub', 'row'), may hold values from -6 to 6
- slope: float32 [4], replicated, may hold values from 0.1 to 1.5
- knee: float32 [3], replicated, may hold values from 0.4 to 2.5
Outputs:
- voltage: float32 [32, 4096, 256], P('sub', 'row')
- flux_state: float32 [32, 64, 256], P('sub', 'row')
Inputs may be any that keep to these rules, and one draw needn't show every extreme that they name: Each pattern has all diagonal blocks present. `line_far`: pairs line ends: the far end of the far end is the line end itself, in another subnetwork, in the same block of 128 line ends; at most 6 line ends of one block lead to one far subnetwork, and that many do in every draw. Both ends of a line have the same delay. `xf_node`: transformer j sits at a node of the same block of 512 nodes as j // 8, never at a line end's node.
All inputs are finite; a program needn't handle non-finite values.
Results may differ from a plain program's by a relative error of at most 0.0055.
Values may be sent and summed in bfloat16 or wider, within the bound.
A program may use at most 64 MiB of HBM per device.

v0:
```python
import jax
import jax.numpy as jnp
from jax import lax
from jax.sharding import PartitionSpec as P


def saturation(flux_now, slope, knee):
    magnitude = jnp.abs(flux_now)
    direction = jnp.sign(flux_now)
    current = slope[0] * flux_now
    for level in range(knee.shape[0]):
        current = current + slope[level + 1] * direction * jnp.maximum(magnitude - knee[level], 0.0)
    return current


def body(source, inverse_z, pattern, line_far, delay, xf_node, wave0, flux0, volt0, slope, knee):
    row_count = inverse_z.shape[1]
    node_count = inverse_z.shape[2]
    block_size = node_count // pattern.shape[2]
    port_dev = line_far.shape[1]
    step_count = source.shape[0]
    n_row = lax.axis_size("row")
    block_mask = jnp.repeat(jnp.repeat(pattern[0], block_size, 0), block_size, 1)
    masked = jnp.where(block_mask > 0, inverse_z[0], jnp.zeros((), jnp.bfloat16))
    port_columns = masked.reshape(row_count, n_row, row_count)[:, :, :port_dev].reshape(
        row_count, n_row * port_dev
    )
    placed = xf_node[0] % row_count
    onehot = (placed[:, None] == jnp.arange(row_count, dtype=jnp.int32)[None, :]).astype(
        jnp.float32
    )
    far_subnet = line_far[0, :, 0]
    far_place = line_far[0, :, 1] % port_dev
    delayed = (delay[0] == 2)[:, None]
    recent = wave0[0, 0]
    earlier = wave0[1, 0]
    flux_state = flux0[0]
    xf_previous = volt0[0]
    voltage = None
    for instant in range(step_count):
        arriving = jnp.where(delayed, earlier, recent)
        current = saturation(flux_state, slope, knee)
        absorbed = jnp.dot(onehot.T, current, precision=lax.Precision.HIGHEST)
        whole_injection = lax.all_gather(
            (source[instant, 0].astype(jnp.float32) - absorbed).astype(jnp.bfloat16),
            "row",
            axis=0,
            tiled=True,
        )
        gathered_waves = lax.all_gather(arriving, "row", axis=0, tiled=True)
        voltage = jnp.dot(masked, whole_injection, preferred_element_type=jnp.float32)
        voltage = voltage + jnp.dot(
            port_columns, gathered_waves, preferred_element_type=jnp.float32
        )
        xf_voltage = jnp.dot(onehot, voltage, precision=lax.Precision.HIGHEST)
        flux_state = flux_state + 0.5 * (xf_voltage + xf_previous)
        xf_previous = xf_voltage
        if instant + 1 < step_count:
            outgoing = (0.5 * voltage[:port_dev] - arriving.astype(jnp.float32)).astype(
                jnp.bfloat16
            )
            everything = lax.all_gather(outgoing, "sub", axis=0, tiled=True)
            incoming = jnp.take(everything, far_subnet * port_dev + far_place, axis=0)
            earlier = recent
            recent = incoming
    return (voltage[None], flux_state[None])


def solution(mesh):
    return jax.shard_map(
        body,
        mesh=mesh,
        in_specs=(
            P(None, "sub", "row", None),
            P("sub", "row", None),
            P("sub", "row", None),
            P("sub", "row", None),
            P("sub", "row"),
            P("sub", "row"),
            P(None, "sub", "row", None),
            P("sub", "row", None),
            P("sub", "row", None),
            P(),
            P(),
        ),
        out_specs=(P("sub", "row", None), P("sub", "row", None)),
        check_vma=False,
    )
```

profile of v0, /device:TPU:2, one launch (start us, length us, event | category | flops | bytes accessed | tf_op | source)
XLA Modules:
  0.0 452.1 jit_solution(11590553098446064711)
XLA Ops:
  7.2 0.0 all-gather.8.cloned.1.call-start
  7.2 0.7 and_select_fusion.1
  7.9 1.4 fusion.150
  9.3 1.4 fusion.151
  10.7 6.6 %fusion = bf16[512,256]{1,0:T(8,128)(2,1)} fusion(bf16[4,1,512,256]{3,2,1,0:T(8,128)(2,1)} %param.13, f32[1,8,256]{2,1,0:T(8,128)} %param.20, s32[8]{0:T(128)S(1)} %and_select_fusion.1, f32[]{:T(128)} %bitcast.13, f32[]{:T(128)} %bitcast.12, f32[]{:T(128)} %bitcast.11, f32[]{:T(128)} %bitcast.10, f32[]{:T(128)} %bitcast.9, f32[]{:T(128)} %bitcast.8, f32[]{:T(128)} %bitcast.5), kind=kOutput, calls=%fused_computation.13 | convolution fusion | flops 13017088 | bytes 532540 | tf_op jit(solution)/shard_map/dot_general | solution.py:43
  17.3 0.0 all-gather.8.cloned.1.call-update
  17.3 0.0 all-gather.10.cloned.1.call-start
  17.4 0.7 compare_bitcast_fusion.1
  18.1 3.5 broadcast_in_dim.48
  21.6 3.9 gt.30
  25.5 3.0 copy.13
  28.5 2.2 copy.14
  30.8 0.1 bitcast_select_fusion.2
  30.9 30.0 %all_gather.34 = bf16[1024,256]{1,0:T(8,128)(2,1)S(1)} all-gather(bf16[128,256]{1,0:T(8,128)(2,1)S(1)} %bitcast_select_fusion.2), channel_id=1, replica_groups=mesh['sub'=32,'row'=8] {'row'}, dimensions={0}, use_global_device_ids=true | all-gather | bytes 589824 | tf_op jit(solution)/shard_map/all_gather | solution.py:50
  60.9 1.2 slice_select_fusion
  62.1 0.9 all-gather.8.cloned.1.call-done
  63.0 4.7 %fusion.149 = f32[512,256]{1,0:T(8,128)S(1)} fusion(bf16[4096,256]{1,0:T(8,128)(2,1)} %all-gather.8.cloned.1.call-done, pred[512,4096]{1,0:T(8,128)(4,1)} %bitcast.127, bf16[1,512,4096]{2,1,0:T(8,128)(2,1)} %param.14), kind=kOutput, calls=%fused_computation.187 | convolution fusion | flops 1075838976 | bytes 8912896 | tf_op jit(solution)/shard_map/dot_general | solution.py:51
  67.7 0.0 copy-start.2
  67.8 0.4 convolution_add_fusion.3
  68.2 0.2 copy-done.4
  68.4 0.0 copy-done.5
  68.4 0.3 fusion.25
  68.7 0.3 copy-done.2
  69.0 5.6 %fusion.1 = bf16[512,256]{1,0:T(8,128)(2,1)} fusion(bf16[4,1,512,256]{3,2,1,0:T(8,128)(2,1)S(1)} %copy-done.2, f32[8,256]{1,0:T(8,128)S(1)} %get-tuple-element.12, s32[8]{0:T(128)S(1)} %and_select_fusion.1, f32[]{:T(128)} %bitcast.13, f32[]{:T(128)} %bitcast.12, f32[]{:T(128)} %bitcast.11, f32[]{:T(128)} %bitcast.10, f32[]{:T(128)} %bitcast.9, f32[]{:T(128)} %bitcast.8, ...), kind=kOutput, calls=%fused_computation.14 | convolution fusion | flops 13017088 | bytes 532540 | tf_op jit(solution)/shard_map/dot_general | solution.py:43
  74.6 0.0 all-gather.10.cloned.1.call-update
  74.6 0.0 all-gather.12.cloned.1.call-start
  74.7 0.7 fusion.20
  75.4 0.0 all-gather.12.cloned.1.call-update
  75.4 0.0 all-gather.14.cloned.1.call-start
  75.5 39.2 %all-gather.10.cloned.1.call-done = bf16[4096,256]{1,0:T(8,128)(2,1)} async-done(((bf16[512,256]{1,0:T(8,128)(2,1)}), bf16[4096,256]{1,0:T(8,128)(2,1)}) %all-gather.10.cloned.1.call-update) | async-done | bytes 2097168 | tf_op jit(solution)/shard_map/all_gather | solution.py:44
  114.7 4.7 %fusion.148 = f32[512,256]{1,0:T(8,128)S(1)} fusion(bf16[4096,256]{1,0:T(8,128)(2,1)} %all-gather.10.cloned.1.call-done, pred[512,4096]{1,0:T(8,128)(4,1)} %bitcast.128, bf16[1,512,4096]{2,1,0:T(8,128)(2,1)} %param.14), kind=kOutput, calls=%fused_computation.186 | convolution fusion | flops 1075838976 | bytes 8912896 | tf_op jit(solution)/shard_map/dot_general | solution.py:51
  119.5 44.8 %all-gather.12.cloned.1.call-done = bf16[4096,256]{1,0:T(8,128)(2,1)} async-done(((bf16[128,256]{1,0:T(8,128)(2,1)}), bf16[4096,256]{1,0:T(8,128)(2,1)}) %all-gather.12.cloned.1.call-update) | async-done | bytes 2097168 | tf_op jit(solution)/shard_map/all_gather | solution.py:62
  164.3 2.6 gather_fusion
  166.9 0.1 bitcast_select_fusion.1
  167.0 26.9 %all_gather.37 = bf16[1024,256]{1,0:T(8,128)(2,1)S(1)} all-gather(bf16[128,256]{1,0:T(8,128)(2,1)S(1)} %bitcast_select_fusion.1), channel_id=1, replica_groups=mesh['sub'=32,'row'=8] {'row'}, dimensions={0}, use_global_device_ids=true | all-gather | bytes 589824 | tf_op jit(solution)/shard_map/all_gather | solution.py:50
  193.9 0.4 convolution_add_fusion.2
  194.3 0.3 fusion.22
  194.6 5.7 %fusion.2 = bf16[512,256]{1,0:T(8,128)(2,1)} fusion(bf16[4,1,512,256]{3,2,1,0:T(8,128)(2,1)S(1)} %copy-done.2, s32[8]{0:T(128)S(1)} %and_select_fusion.1, f32[]{:T(128)} %bitcast.13, f32[]{:T(128)} %bitcast.12, f32[]{:T(128)} %bitcast.11, f32[]{:T(128)} %bitcast.10, f32[]{:T(128)} %bitcast.9, f32[]{:T(128)} %bitcast.8, f32[]{:T(128)} %bitcast.5, ...), kind=kOutput, calls=%fused_computation.15 | convolution fusion | flops 13023232 | bytes 548924 | tf_op jit(solution)/shard_map/dot_general | solution.py:43
  200.2 0.0 all-gather.14.cloned.1.call-update
  200.3 0.0 all-gather.16.cloned.1.call-start
  200.3 0.6 fusion.18
  200.9 0.0 all-gather.16.cloned.1.call-update
  201.0 0.2 all-gather.18.cloned.1.call-start
  201.2 38.6 %all-gather.14.cloned.1.call-done = bf16[4096,256]{1,0:T(8,128)(2,1)} async-done(((bf16[512,256]{1,0:T(8,128)(2,1)}), bf16[4096,256]{1,0:T(8,128)(2,1)}) %all-gather.14.cloned.1.call-update) | async-done | bytes 2097168 | tf_op jit(solution)/shard_map/all_gather | solution.py:44
  239.8 4.7 %fusion.147 = f32[512,256]{1,0:T(8,128)S(1)} fusion(bf16[4096,256]{1,0:T(8,128)(2,1)} %all-gather.14.cloned.1.call-done, pred[512,4096]{1,0:T(8,128)(4,1)} %bitcast.129, bf16[1,512,4096]{2,1,0:T(8,128)(2,1)} %param.14), kind=kOutput, calls=%fused_computation.185 | convolution fusion | flops 1075838976 | bytes 8912896 | tf_op jit(solution)/shard_map/dot_general | solution.py:51
  244.6 44.7 %all-gather.16.cloned.1.call-done = bf16[4096,256]{1,0:T(8,128)(2,1)} async-done(((bf16[128,256]{1,0:T(8,128)(2,1)}), bf16[4096,256]{1,0:T(8,128)(2,1)}) %all-gather.16.cloned.1.call-update) | async-done | bytes 2097168 | tf_op jit(solution)/shard_map/all_gather | solution.py:62
  289.2 2.6 gather_fusion.1
  291.8 0.1 broadcast_select_fusion.2
  291.9 26.9 %all_gather.40 = bf16[1024,256]{1,0:T(8,128)(2,1)S(1)} all-gather(bf16[128,256]{1,0:T(8,128)(2,1)S(1)} %broadcast_select_fusion.2), channel_id=1, replica_groups=mesh['sub'=32,'row'=8] {'row'}, dimensions={0}, use_global_device_ids=true | all-gather | bytes 589824 | tf_op jit(solution)/shard_map/all_gather | solution.py:50
  318.8 0.4 convolution_add_fusion.1
  319.2 0.3 fusion.21
  319.5 5.7 %fusion.3 = bf16[512,256]{1,0:T(8,128)(2,1)} fusion(bf16[4,1,512,256]{3,2,1,0:T(8,128)(2,1)S(1)} %copy-done.2, s32[8]{0:T(128)S(1)} %and_select_fusion.1, f32[]{:T(128)} %bitcast.13, f32[]{:T(128)} %bitcast.12, f32[]{:T(128)} %bitcast.11, f32[]{:T(128)} %bitcast.10, f32[]{:T(128)} %bitcast.9, f32[]{:T(128)} %bitcast.8, f32[]{:T(128)} %bitcast.5, ...), kind=kOutput, calls=%fused_computation.16 | convolution fusion | flops 13029376 | bytes 557116 | tf_op jit(solution)/shard_map/dot_general | solution.py:43
  325.2 0.0 all-gather.18.cloned.1.call-update
  325.2 0.0 all-gather.20.cloned.1.call-start
  325.2 0.6 fusion.16
  325.9 0.1 all-gather.20.cloned.1.call-update
  326.0 38.8 %all-gather.18.cloned.1.call-done = bf16[4096,256]{1,0:T(8,128)(2,1)} async-done(((bf16[512,256]{1,0:T(8,128)(2,1)}), bf16[4096,256]{1,0:T(8,128)(2,1)}) %all-gather.18.cloned.1.call-update) | async-done | bytes 2097168 | tf_op jit(solution)/shard_map/all_gather | solution.py:44
  364.8 4.7 %fusion.146 = f32[512,256]{1,0:T(8,128)S(1)} fusion(bf16[4096,256]{1,0:T(8,128)(2,1)} %all-gather.18.cloned.1.call-done, pred[512,4096]{1,0:T(8,128)(4,1)} %bitcast.130, bf16[1,512,4096]{2,1,0:T(8,128)(2,1)} %param.14), kind=kOutput, calls=%fused_computation.184 | convolution fusion | flops 1075838976 | bytes 8912896 | tf_op jit(solution)/shard_map/dot_general | solution.py:51
  369.5 44.8 %all-gather.20.cloned.1.call-done = bf16[4096,256]{1,0:T(8,128)(2,1)} async-done(((bf16[128,256]{1,0:T(8,128)(2,1)}), bf16[4096,256]{1,0:T(8,128)(2,1)}) %all-gather.20.cloned.1.call-update) | async-done | bytes 2097168 | tf_op jit(solution)/shard_map/all_gather | solution.py:62
  414.3 2.6 gather_fusion.2
  416.9 0.1 select_select_fusion
  417.0 26.9 %all_gather.43 = bf16[1024,256]{1,0:T(8,128)(2,1)S(1)} all-gather(bf16[128,256]{1,0:T(8,128)(2,1)S(1)} %select_select_fusion), channel_id=1, replica_groups=mesh['sub'=32,'row'=8] {'row'}, dimensions={0}, use_global_device_ids=true | all-gather | bytes 589824 | tf_op jit(solution)/shard_map/all_gather | solution.py:50
  443.9 0.4 convolution_add_fusion
  444.3 0.9 fusion.6
  (16 shorter events, 0.1 us)
Async XLA Ops:
  7.2 55.8 %all-gather.8.cloned.1.call-start = ((), (), s32[]{:S(2)}) async-start(), calls=%async_computation | async-start | bytes 2359296 | tf_op jit(solution)/shard_map/all_gather | solution.py:44
  17.3 97.4 %all-gather.10.cloned.1.call-start = ((), (), s32[]{:S(2)}) async-start(), calls=%async_computation.1 | async-start | bytes 2359296 | tf_op jit(solution)/shard_map/all_gather | solution.py:44
  25.5 3.0 copy-start
  28.5 2.2 copy-start.7
  28.5 2.3 copy-start.3
  67.7 0.7 copy-start.4
  67.7 0.7 copy-start.5
  67.7 1.2 copy-start.2
  67.7 7.7 %copy-start.6 = (s32[1,128,2]{1,2,0:T(2,128)S(1)}, s32[1,128,2]{1,2,0:T(2,128)}, u32[]{:S(2)}) copy-start(s32[1,128,2]{1,2,0:T(2,128)} %param.16) | copy-start | bytes 3076
  74.6 89.6 %all-gather.12.cloned.1.call-start = ((), (), s32[]{:S(2)}) async-start(), calls=%async_computation.2 | async-start | bytes 2162688 | tf_op jit(solution)/shard_map/all_gather | solution.py:62
  75.4 164.4 %all-gather.14.cloned.1.call-start = ((), (), s32[]{:S(2)}) async-start(), calls=%async_computation.3 | async-start | bytes 2359296 | tf_op jit(solution)/shard_map/all_gather | solution.py:44
  200.3 89.0 %all-gather.16.cloned.1.call-start = ((), (), s32[]{:S(2)}) async-start(), calls=%async_computation.4 | async-start | bytes 2162688 | tf_op jit(solution)/shard_map/all_gather | solution.py:62
  201.0 163.8 %all-gather.18.cloned.1.call-start = ((), (), s32[]{:S(2)}) async-start(), calls=%async_computation.5 | async-start | bytes 2359296 | tf_op jit(solution)/shard_map/all_gather | solution.py:44
  325.2 89.1 %all-gather.20.cloned.1.call-start = ((), (), s32[]{:S(2)}) async-start(), calls=%async_computation.6 | async-start | bytes 2162688 | tf_op jit(solution)/shard_map/all_gather | solution.py:62
  444.3 0.9 copy-start.1
Sparse Core Ops, SparseCore 0:
  17.5 45.4 all-gather.7
  74.7 39.9 all-gather.9
  117.3 46.9 all-gather.11
  200.4 39.4 all-gather.13
  242.2 46.9 all-gather.15
  325.3 39.4 all-gather.17
  367.3 46.9 all-gather.19
where the time goes:
time: 453 us; the launch traced here: 452 us
  waiting for transfers between devices  252 us (56%)
  blocking collectives  111 us (25%)
  matrix products  45.9 us (10%)
  local copies, waits for them, and re-layouts  23.9 us (5%)
  between operations  14.3 us (3%)
  other arithmetic  4.97 us (1%)
    all_gather x3, waiting for transfers between devices, body(): everything = lax.all_gather(outgoing, 'sub', axis=0, tiled=True)  134 us
    all_gather x4, waiting for transfers between devices, body(): lax.all_gather((source[instant, 0].astype(jnp.float32) - absorbed).astype...  118 us
    all_gather x4, blocking collectives, body(): gathered_waves = lax.all_gather(arriving, 'row', axis=0, tiled=True)  111 us
    dot_general x4, matrix products, body(): absorbed = jnp.dot(onehot.T, current, precision=lax.Precision.HIGHEST)  23.6 us
    dot_general x4, matrix products, body(): jnp.dot(masked, whole_injection, preferred_element_type=jnp.float32)  18.9 us
  transfers between devices with their start and end apart: 7, of which 7 were waited for; matrix products, arithmetic and copies ran while one was open for 7% of the time, Pallas kernels for 0%

commit v1 on v0

v1 whole, which is shorter than its diff:
```python
import functools

import jax
import jax.numpy as jnp
from jax import lax
from jax.experimental import pallas as pl
from jax.experimental.pallas import tpu as pltpu
from jax.sharding import PartitionSpec as P

MESH = pl.DeviceIdType.MESH
BF = jnp.bfloat16
F32 = jnp.float32
HALF = 128
SLOTS = 8


def dot(a, b):
    return jnp.dot(a, b, preferred_element_type=F32)


def dot_t(a, b):
    return lax.dot_general(a, b, (((1,), (1,)), ((), ())), preferred_element_type=F32)


def kernel(
    n_sub, n_row, rows, ports, xfs, steps, block,
    source, z, pattern, far, delay, xf, wave0, flux0, volt0, slope, knee,
    vout, fout,
    zm, src, zc, zx, stat, y, rs_send, rs_recv, xs, xr, pk, un, s3, d3, zx3, xfi, xfr, vacc, wrec, wear, warr, cur,
    load_sem, z_send, z_recv, rs_ssem, rs_rsem, x_ssem, x_rsem, s3_ssem, s3_rsem, d3_ssem, d3_rsem, i_ssem, i_rsem,
):
    me = lax.axis_index("row")
    sub = lax.axis_index("sub")
    last = steps - 1
    other = rows - ports
    xr2 = 2 * xfs
    prow = ports + xr2
    scen = 2 * HALF
    n_hop = n_row // 2

    def at_row(d):
        return (sub, lax.rem(me + d + 2 * n_row, n_row))

    def row_of(d):
        return lax.rem(me + d + 2 * n_row, n_row)

    def remote(a, b, ss, rs, dev):
        return pltpu.make_async_remote_copy(
            src_ref=a, dst_ref=b, send_sem=ss, recv_sem=rs, device_id=dev, device_id_type=MESH
        )

    ld_ports = pltpu.make_async_copy(z.at[pl.ds(0, ports)], zm.at[pl.ds(0, ports)], load_sem.at[0])
    ld_rest = pltpu.make_async_copy(z.at[pl.ds(ports, other)], zm.at[pl.ds(ports, other)], load_sem.at[1])
    ld_src = pltpu.make_async_copy(source, src, load_sem.at[2])
    ld_ports.start()
    ld_rest.start()
    ld_src.start()
    barrier = pltpu.get_barrier_semaphore()
    for d in range(1, n_row):
        pl.semaphore_signal(barrier, inc=1, device_id=at_row(d), device_id_type=MESH)

    def greet(i, c):
        pl.semaphore_signal(
            barrier, inc=1, device_id=(lax.rem(sub + i, n_sub), me), device_id_type=MESH
        )
        return c

    lax.fori_loop(1, n_sub, greet, 0)

    ri = lax.broadcasted_iota(jnp.int32, (xr2, rows), 0)
    li = lax.broadcasted_iota(jnp.int32, (xr2, rows), 1)
    oh = jnp.zeros((xr2, rows), F32)
    bi = lax.broadcasted_iota(jnp.int32, (xfs, 128), 0)
    idx = jnp.zeros((xfs, 128), jnp.int32)
    for j in range(xfs):
        node = xf[0, j] & (rows - 1)
        oh = jnp.where((lax.rem(ri, xfs) == j) & (li == node), 1.0, oh)
        idx = jnp.where(bi == j, node, idx)
    oh = oh.astype(BF)
    node_col = idx[:, 0:1]
    node_row = jnp.zeros((1, xfs), jnp.int32)
    lane = lax.broadcasted_iota(jnp.int32, (1, xfs), 1)
    for j in range(xfs):
        node_row = jnp.where(lane == j, xf[0, j] & (rows - 1), node_row)
    shared = node_col == node_row
    ahead = lax.broadcasted_iota(jnp.int32, (xfs, xfs), 1) < lax.broadcasted_iota(jnp.int32, (xfs, xfs), 0)
    first = jnp.sum(jnp.where(shared & ahead, 1, 0), axis=1, keepdims=True) == 0
    xfi[...] = idx
    xfr[me] = idx

    def mask_rows(lo, count, brow):
        def one(b, c):
            m = jnp.where(pattern[brow, b] > 0, 1.0, 0.0).astype(F32)
            mv = jnp.full((1, block), m, F32).astype(BF)
            cols = pl.ds(pl.multiple_of(b * block, block), block)
            zm[lo : lo + count, cols] = zm[lo : lo + count, cols] * mv
            return c

        lax.fori_loop(0, n_row * rows // block, one, 0)

    ld_ports.wait()
    mask_rows(0, ports, 0)
    ld_rest.wait()
    mask_rows(ports, block - ports, 0)
    for b in range(1, rows // block):
        mask_rows(b * block, block, b)

    def pick(c, carry):
        cols = pl.ds(pl.multiple_of(c * rows, rows), rows)
        zm[rows : rows + xr2, cols] = dot(oh, zm[0:rows, cols]).astype(BF)
        return carry

    lax.fori_loop(0, n_row, pick, 0)

    pl.semaphore_wait(barrier, n_row - 1 + n_sub - 1)

    order = [n_hop]
    for d in range(n_hop - 1, 0, -1):
        order += [d, n_row - d]
    z_copies = {}
    for d in order:
        cols = pl.ds(pl.multiple_of(row_of(d) * rows, rows), rows)
        a = remote(zm.at[pl.ds(0, ports), cols], zc.at[me, pl.ds(0, ports)], z_send.at[0, d], z_recv.at[0, d], at_row(d))
        b = remote(zm.at[pl.ds(rows, xr2), cols], zc.at[me, pl.ds(ports, xr2)], z_send.at[1, d], z_recv.at[1, d], at_row(d))
        a.start()
        b.start()
        z_copies[d] = (a, b)
    i_copies = []
    for d in range(1, n_row):
        c = remote(xfi, xfr.at[me], i_ssem.at[d], i_rsem.at[d], at_row(d))
        c.start()
        i_copies.append(c)

    eye = lax.broadcasted_iota(jnp.int32, (ports, ports), 0) == lax.broadcasted_iota(jnp.int32, (ports, ports), 1)
    before = lax.broadcasted_iota(jnp.int32, (ports, ports), 0) < lax.broadcasted_iota(jnp.int32, (ports, ports), 1)
    fs_col = far[:, 0:1]
    fp_col = far[:, 1:2]
    fs_row = jnp.sum(jnp.where(eye, fs_col, 0), axis=0, keepdims=True)
    fp_row = jnp.sum(jnp.where(eye, fp_col, 0), axis=0, keepdims=True)
    same = fs_col == fs_row
    rank_row = jnp.sum(jnp.where(same & before, 1, 0), axis=0, keepdims=True)
    rank_col = jnp.sum(jnp.where(same & (fp_row < fp_col), 1, 0), axis=1, keepdims=True)
    dl_col = jnp.sum(jnp.where(eye, delay[...], 0), axis=1, keepdims=True)
    late = dl_col == 2
    n_slot = 2 * SLOTS * n_sub
    place_row = fs_row * (2 * SLOTS) + rank_row
    place_col = fs_col * (2 * SLOTS) + rank_col
    for h in range(2):
        pi = lax.broadcasted_iota(jnp.int32, (n_slot, ports), 0)
        pk[:, h * ports : (h + 1) * ports] = jnp.where(pi == place_row + h * SLOTS, 1.0, 0.0).astype(BF)
        ui = lax.broadcasted_iota(jnp.int32, (ports, n_slot), 1)
        un[h * ports : (h + 1) * ports, :] = jnp.where(ui == place_col + h * SLOTS, 1.0, 0.0).astype(BF)
    own_slots = pl.ds(pl.multiple_of(sub * 2 * SLOTS, 2 * SLOTS), 2 * SLOTS)
    for t in range(last):
        xr[t, own_slots, :] = jnp.zeros((2 * SLOTS, HALF), BF)

    wrec[...] = wave0[0].astype(F32)
    wear[...] = wave0[1].astype(F32)

    def currents(flux, at_xf):
        total = slope[0] * flux
        for level in range(3):
            total = total + slope[level + 1] * (
                jnp.maximum(flux - knee[level], 0.0) + jnp.minimum(flux + knee[level], 0.0)
            )
        absorbed = jnp.zeros_like(total)
        for j in range(xfs):
            absorbed = absorbed + jnp.where(shared[:, j : j + 1], total[j : j + 1], 0.0)
        inject = (at_xf - absorbed).astype(BF).astype(F32)
        delta = jnp.where(first, inject - at_xf, 0.0)
        high = delta.astype(BF).astype(F32)
        return jnp.concatenate([high, delta - high], axis=0)

    def begin(t, flux):
        warr[...] = jnp.where(late, wear[...], wrec[...])
        cur[...] = currents(flux, dot(oh, src[t])[0:xfs]).astype(BF)

    flux = flux0[...]
    xprev = volt0[...]
    ld_src.wait()
    begin(0, flux)

    own_cols = pl.ds(pl.multiple_of(me * rows, rows), rows)
    zc[me, 0:ports] = zm[0:ports, own_cols]
    zc[me, ports:prow] = zm[rows : rows + xr2, own_cols]
    s3[me] = src[last, ports:rows, :]

    def products(r):
        zr = zc[r]
        zx[r] = dot_t(zr, oh).astype(BF)
        for t in range(last):
            stat[t, r] = dot(zr, src[t])

    def add_dynamic(t, r):
        y[r] = stat[t, r] + dot(zc[r, :, 0:ports], warr[...].astype(BF)) + dot(zx[r], cur[...])

    first_dir = jnp.where(lax.rem(me, n_hop) < n_hop // 2, 1, 0)

    def both(v):
        v = v.astype(F32)
        return v[0:xfs] + v[xfs:]

    def reduce_scatter(t, ready):
        copies = []

        def push(dirn, sign, dest, k, h, wait):
            lanes = pl.ds(pl.multiple_of(h * HALF, HALF), HALF)
            acc_p = y[dest, 0:ports, lanes]
            acc_x = y[dest, ports : ports + xfs, lanes]
            if wait:
                got = rs_recv.at[t, dirn, k - 1, h]
                remote(got, got, rs_ssem.at[t, dirn, k - 1, h], rs_rsem.at[t, dirn, k - 1, h], at_row(sign)).wait_recv()
                acc_p = acc_p + got[0:ports].astype(F32)
                acc_x = acc_x + both(got[ports:prow])
            high = acc_x.astype(BF).astype(F32)
            rs_send[t, dirn, k, h, 0:ports] = acc_p.astype(BF)
            rs_send[t, dirn, k, h, ports:prow] = jnp.concatenate([high, acc_x - high], axis=0).astype(BF)
            c = remote(
                rs_send.at[t, dirn, k, h], rs_recv.at[t, dirn, k, h], rs_ssem.at[t, dirn, k, h], rs_rsem.at[t, dirn, k, h], at_row(sign)
            )
            c.start()
            copies.append(c)

        for k in range(n_hop):
            ready(n_hop - k)
            for j in range(2):
                dirn = jnp.bitwise_xor(first_dir, j)
                sign = 1 - 2 * dirn
                dest = row_of(sign * (n_hop - k))
                if k == 0:
                    push(dirn, sign, dest, k, dirn, False)
                elif k == 1:
                    push(dirn, sign, dest, k, 1 - dirn, False)
            for j in range(2):
                dirn = jnp.bitwise_xor(first_dir, j)
                sign = 1 - 2 * dirn
                dest = row_of(sign * (n_hop - k))
                if k == 1:
                    push(dirn, sign, dest, k, dirn, True)
                elif k > 1:
                    for h in range(2):
                        push(dirn, sign, dest, k, h, True)
        ready(0)
        for dirn in range(2):
            for h in range(2):
                got = rs_recv.at[t, dirn, n_hop - 1, h]
                remote(
                    got, got, rs_ssem.at[t, dirn, n_hop - 1, h], rs_rsem.at[t, dirn, n_hop - 1, h], at_row(1)
                ).wait_recv()
        at_ports, at_xfs = [], []
        for h in range(2):
            lanes = slice(h * HALF, (h + 1) * HALF)
            left, right = rs_recv.at[t, 0, n_hop - 1, h], rs_recv.at[t, 1, n_hop - 1, h]
            at_ports.append(y[me, 0:ports, lanes] + left[0:ports].astype(F32) + right[0:ports].astype(F32))
            at_xfs.append(y[me, ports : ports + xfs, lanes] + both(left[ports:prow]) + both(right[ports:prow]))
        return at_ports, at_xfs, copies

    def gather_hop(buf, own, k, ssem, rsem, cut):
        made = []
        n = buf.shape[1]
        for dirn in range(2):
            sign = 1 - 2 * dirn
            c = row_of(-sign * k)
            if k < n_hop - 1:
                part = pl.ds(0, n)
            else:
                part = pl.ds(0, cut) if dirn == 0 else pl.ds(cut, n - cut)
            cp = remote(buf.at[c, part], buf.at[c, part], ssem.at[dirn, k], rsem.at[dirn, k], at_row(sign))
            cp.start()
            made.append(cp)
        return made

    def gather_wait(made):
        for cp in made:
            cp.wait_recv()

    def add_static(c):
        lo = pl.multiple_of(c * rows + ports, ports)
        vacc[...] += dot(zm[:, pl.ds(lo, other)], s3[c])

    def add_last(c):
        lo = pl.multiple_of(c * rows, rows)
        vacc[...] += dot(zm[:, pl.ds(lo, ports)], d3[c, 0:ports]) + dot(zx3[c], d3[c, ports:prow])

    sends = []
    s3_hops = []
    for t in range(last):
        if t == 0:

            def ready(d):
                for e in (d, n_row - d) if 0 < d < n_hop else (d,):
                    if e:
                        f = n_row - e
                        r = row_of(e)
                        remote(zc.at[r, pl.ds(0, ports)], zc.at[r, pl.ds(0, ports)], z_send.at[0, f], z_recv.at[0, f], at_row(1)).wait_recv()
                        remote(zc.at[r, pl.ds(ports, xr2)], zc.at[r, pl.ds(ports, xr2)], z_send.at[1, f], z_recv.at[1, f], at_row(1)).wait_recv()
                        products(r)
                        add_dynamic(0, r)

            products(me)
            add_dynamic(0, me)
        else:

            def ready(d, t=t):
                for e in (d, n_row - d) if 0 < d < n_hop else (d,):
                    add_dynamic(t, row_of(e))

        at_ports, at_xfs, copies = reduce_scatter(t, ready)
        sends += copies
        xv = jnp.concatenate(at_xfs, axis=1)
        flux = flux + 0.5 * (xv + xprev)
        xprev = xv
        out = jnp.concatenate(
            [(0.5 * at_ports[h] - warr[:, h * HALF : (h + 1) * HALF]) for h in range(2)], axis=0
        ).astype(BF)
        xs[t] = dot(pk[...], out).astype(BF)

        def put(i, c, t=t):
            p = lax.rem(sub + i, n_sub)
            remote(
                xs.at[t, pl.ds(pl.multiple_of(p * 2 * SLOTS, 2 * SLOTS), 2 * SLOTS)],
                xr.at[t, own_slots],
                x_ssem.at[t],
                x_rsem.at[t],
                (p, me),
            ).start()
            return c

        lax.fori_loop(1, n_sub, put, 0)
        if s3_hops:
            gather_wait(s3_hops[-1])
        s3_hops.append(gather_hop(s3, None, t, s3_ssem, s3_rsem, other // 2))
        if t == 0:
            vacc[...] = jnp.zeros_like(vacc)
            add_static(me)
            for d in range(1, n_row):
                c = row_of(-d)
                remote(xfr.at[c], xfr.at[c], i_ssem.at[d], i_rsem.at[d], at_row(1)).wait_recv()

            def columns(c, carry):
                node = xfr[c][:, 0:1]
                hot = jnp.where(lax.broadcasted_iota(jnp.int32, (xfs, rows), 1) == node, 1.0, 0.0)
                hot = jnp.concatenate([hot, hot], axis=0).astype(BF)
                cols = pl.ds(pl.multiple_of(c * rows, rows), rows)
                zx3[c] = dot_t(zm[:, cols], hot).astype(BF)
                return carry

            lax.fori_loop(0, n_row, columns, 0)
        else:
            add_static(row_of(-t))
            add_static(row_of(t))
        total = pl.ds(0, (n_sub - 1) * 2 * SLOTS)
        pltpu.make_async_copy(xs.at[t, total], xr.at[t, total], x_rsem.at[t]).wait()
        inc = dot(un[...], xr[t])
        wear[...] = wrec[...]
        wrec[...] = jnp.concatenate([inc[0:ports], inc[ports : 2 * ports]], axis=1)
        begin(t + 1, flux)

    d3[me, 0:ports] = (src[last, 0:ports, :].astype(F32) + warr[...]).astype(BF)
    d3[me, ports:prow] = cur[...]
    d3_hops = [gather_hop(d3, None, 0, d3_ssem, d3_rsem, 64)]
    gather_wait(s3_hops[-1])
    s3_hops.append(gather_hop(s3, None, n_hop - 1, s3_ssem, s3_rsem, other // 2))
    add_last(me)
    add_static(row_of(-(n_hop - 1)))
    add_static(row_of(n_hop - 1))
    for k in range(1, n_hop):
        gather_wait(d3_hops[-1])
        d3_hops.append(gather_hop(d3, None, k, d3_ssem, d3_rsem, 64))
        add_last(row_of(-k))
        add_last(row_of(k))
    gather_wait(s3_hops[-1])
    add_static(row_of(n_hop))
    gather_wait(d3_hops[-1])
    add_last(row_of(n_hop))
    vout[...] = vacc[0:rows]
    fout[...] = flux + 0.5 * (vacc[rows : rows + xfs] + xprev)

    for d in order:
        for cp in z_copies[d]:
            cp.wait_send()
    for cp in i_copies + sends:
        cp.wait_send()
    for made in s3_hops + d3_hops:
        for cp in made:
            cp.wait_send()
    for t in range(last):
        total = pl.ds(0, (n_sub - 1) * 2 * SLOTS)
        pltpu.make_async_copy(xs.at[t, total], xr.at[t, total], x_ssem.at[t]).wait()


def body(source, inverse_z, pattern, line_far, delay, xf_node, wave0, flux0, volt0, slope, knee):
    steps, _, rows, scen = source.shape
    nodes = inverse_z.shape[2]
    ports = line_far.shape[1]
    xfs = xf_node.shape[1]
    n_sub, n_row = lax.axis_size("sub"), lax.axis_size("row")
    block = nodes // pattern.shape[2]
    last = steps - 1
    xr2 = 2 * xfs
    prow = ports + xr2
    n_hop = n_row // 2
    other = rows - ports
    n_slot = 2 * SLOTS * n_sub
    vmem = pl.BlockSpec(memory_space=pltpu.VMEM)
    smem = pl.BlockSpec(memory_space=pltpu.SMEM)
    hbm = pl.BlockSpec(memory_space=pl.ANY)
    dma = pltpu.SemaphoreType.DMA
    voltage, flux = pl.pallas_call(
        functools.partial(kernel, n_sub, n_row, rows, ports, xfs, steps, block),
        out_shape=(
            jax.ShapeDtypeStruct((rows, scen), F32),
            jax.ShapeDtypeStruct((xfs, scen), F32),
        ),
        in_specs=[hbm, hbm, smem, vmem, vmem, smem, vmem, vmem, vmem, smem, smem],
        out_specs=(vmem, vmem),
        scratch_shapes=[
            pltpu.VMEM((rows + xr2, nodes), BF),
            pltpu.VMEM((steps, rows, scen), BF),
            pltpu.VMEM((n_row, prow, rows), BF),
            pltpu.VMEM((n_row, prow, xr2), BF),
            pltpu.VMEM((last, n_row, prow, scen), F32),
            pltpu.VMEM((n_row, prow, scen), F32),
            pltpu.VMEM((last, 2, n_hop, 2, prow, HALF), BF),
            pltpu.VMEM((last, 2, n_hop, 2, prow, HALF), BF),
            pltpu.VMEM((last, n_slot, HALF), BF),
            pltpu.VMEM((last, n_slot, HALF), BF),
            pltpu.VMEM((n_slot, 2 * ports), BF),
            pltpu.VMEM((2 * ports, n_slot), BF),
            pltpu.VMEM((n_row, other, scen), BF),
            pltpu.VMEM((n_row, prow, scen), BF),
            pltpu.VMEM((n_row, rows + xr2, xr2), BF),
            pltpu.VMEM((xfs, 128), jnp.int32),
            pltpu.VMEM((n_row, xfs, 128), jnp.int32),
            pltpu.VMEM((rows + xr2, scen), F32),
            pltpu.VMEM((ports, scen), F32),
            pltpu.VMEM((ports, scen), F32),
            pltpu.VMEM((ports, scen), F32),
            pltpu.VMEM((xr2, scen), BF),
            dma((3,)),
            dma((2, n_row)),
            dma((2, n_row)),
            dma((last, 2, n_hop, 2)),
            dma((last, 2, n_hop, 2)),
            dma((last,)),
            dma((last,)),
            dma((2, n_hop)),
            dma((2, n_hop)),
            dma((2, n_hop)),
            dma((2, n_hop)),
            dma((n_row,)),
            dma((n_row,)),
        ],
        compiler_params=pltpu.CompilerParams(
            collective_id=0, has_side_effects=True, vmem_limit_bytes=48 * 2**20
        ),
        name="grid_steps",
    )(
        source.reshape(steps, rows, scen),
        inverse_z.reshape(rows, nodes),
        pattern.reshape(pattern.shape[1:]),
        line_far.reshape(ports, 2),
        delay,
        xf_node,
        wave0.reshape(2, ports, scen),
        flux0.reshape(xfs, scen),
        volt0.reshape(xfs, scen),
        slope,
        knee,
    )
    return (voltage[None], flux[None])


def solution(mesh):
    return jax.shard_map(
        body,
        mesh=mesh,
        in_specs=(
            P(None, "sub", "row", None),
            P("sub", "row", None),
            P("sub", "row", None),
            P("sub", "row", None),
            P("sub", "row"),
            P("sub", "row"),
            P(None, "sub", "row", None),
            P("sub", "row", None),
            P("sub", "row", None),
            P(),
            P(),
        ),
        out_specs=(P("sub", "row", None), P("sub", "row", None)),
        check_vma=False,
    )
```

time: 453 us -> 125 us (0.28)
  waiting for transfers between devices: 252 us -> 0 us
  Pallas kernels: 0 us -> 113 us
  blocking collectives: 111 us -> 0 us
  matrix products: 45.9 us -> 0 us
  between operations: 14.3 us -> 0.65 us
  local copies, waits for them, and re-layouts: 23.9 us -> 11.2 us
  other arithmetic: 4.97 us -> 0 us
    all_gather x7 -> x0, waiting for transfers between devices: 252 us -> none  [the longest x3 134 us: body(): everything = lax.all_gather(outgoing, 'sub', axis=0, tiled=True)]
    pallas_call x0 -> x1, Pallas kernels: none -> 113 us  [body(): pl.pallas_call(functools.partial(kernel, n_sub, n_row, rows, ports, xfs,...]
    all_gather x4 -> x0, blocking collectives: 111 us -> none  [body(): gathered_waves = lax.all_gather(arriving, 'row', axis=0, tiled=True)]
    dot_general x16 -> x0, matrix products: 45.9 us -> none  [the longest x4 23.6 us: body(): absorbed = jnp.dot(onehot.T, current, precision=lax.Precision.HIGHEST)]
    gather x3 -> x0, local copies, waits for them, and re-layouts: 7.84 us -> none  [body(): incoming = jnp.take(everything, far_subnet * port_dev + far_place, axis=0)]
    unnamed x18 -> x23, local copies, waits for them, and re-layouts: 5.78 us -> 11.2 us
  transfers between devices with their start and end apart: 7 -> 0, of which waited for: 7 -> 0; matrix products, arithmetic and copies ran while one was open for 7% -> 0% of each run, Pallas kernels for 0% -> 0%
where the time goes in v1:
time: 125 us
  Pallas kernels  113 us (90%)
  local copies, waits for them, and re-layouts  11.2 us (9%)
    pallas_call x1, Pallas kernels, body(): pl.pallas_call(functools.partial(kernel, n_sub, n_row, rows, ports, xfs,...  113 us
    unnamed x23, local copies, waits for them, and re-layouts  11.2 us

profile of v1, /device:TPU:2, one launch (start us, length us, event | category | flops | bytes accessed | tf_op | source)
XLA Modules:
  0.0 124.6 jit_solution(9866302865122343717)
XLA Ops:
  0.6 0.8 copy.13
  1.4 0.0 copy-start
  1.4 2.2 %copy-done = bf16[1,512,4096]{2,1,0:T(8,128)(2,1)S(1)} copy-done((bf16[1,512,4096]{2,1,0:T(8,128)(2,1)S(1)}, bf16[1,512,4096]{2,1,0:T(8,128)(2,1)}, u32[]{:S(2)}) %copy-start) | copy-done | bytes 4194328
  3.6 0.0 copy-start.1
  3.6 1.2 copy-done.1
  4.8 0.0 copy-start.2
  4.8 0.9 copy-done.2
  5.7 0.0 copy-start.3
  5.7 0.7 copy-done.3
  6.4 0.0 copy-start.4
  6.4 0.7 copy-done.4
  7.1 0.0 copy-start.5
  7.1 0.7 copy-done.5
  7.8 0.0 copy-start.6
  7.8 0.7 copy-done.6
  8.5 0.0 copy-start.7
  8.5 0.7 copy-done.7
  9.1 0.0 copy-start.8
  9.1 0.7 copy-done.8
  9.8 0.0 copy-start.9
  9.8 0.7 copy-done.9
  10.4 112.7 %grid_steps.1 = (f32[512,256]{1,0:T(8,128)S(1)}, f32[8,256]{1,0:T(8,128)S(1)}) custom-call(bf16[4,512,256]{2,1,0:T(8,128)(2,1)S(1)} %bitcast.10, bf16[512,4096]{1,0:T(8,128)(2,1)S(1)} %bitcast.9, s32[2,16]{1,0:T(2,128)S(1)} %bitcast.17, s32[128,2]{1,0:T(8,128)S(1)} %bitcast.12, s32[1,128]{1,0:T(1,128)S(1)} %copy-done.6, s32[1,8]{1,0:T(1,128)S(1)} %copy-done.7, ...), custom_call_target="tpu_custom_call" | custom-call | tf_op jit(solution)/shard_map/grid_steps/pallas_call | solution.py:409
  123.2 0.8 copy.16
  124.0 0.6 copy.17
Async XLA Ops:
  1.4 2.2 %copy-start = (bf16[1,512,4096]{2,1,0:T(8,128)(2,1)S(1)}, bf16[1,512,4096]{2,1,0:T(8,128)(2,1)}, u32[]{:S(2)}) copy-start(bf16[1,512,4096]{2,1,0:T(8,128)(2,1)} %param.12) | copy-start | bytes 12582916
  3.6 1.2 copy-start.1
  4.8 0.9 copy-start.2
  5.7 0.7 copy-start.3
  6.4 0.7 copy-start.4
  7.1 0.7 copy-start.5
  7.8 0.7 copy-start.6
  8.5 0.7 copy-start.7
  9.1 0.7 copy-start.8
  9.8 0.7 copy-start.9

commit v2 on v1

v2 whole, which is shorter than its diff:
```python
import functools

import jax
import jax.numpy as jnp
from jax import lax
from jax.experimental import pallas as pl
from jax.experimental.pallas import tpu as pltpu
from jax.sharding import PartitionSpec as P

MESH = pl.DeviceIdType.MESH
BF = jnp.bfloat16
F32 = jnp.float32
HALF = 128
SLOTS = 8


def dot(a, b):
    return jnp.dot(a, b, preferred_element_type=F32)


def dot_t(a, b):
    return lax.dot_general(a, b, (((1,), (1,)), ((), ())), preferred_element_type=F32)


def kernel(
    n_sub, n_row, rows, ports, xfs, steps, block,
    source, z, pattern_in, far_in, delay_in, xf_in, wave0_in, flux0_in, volt0_in, slope_in, knee_in,
    vout, fout,
    pattern, far, delay, xf, wave0, flux0, volt0, slope, knee,
    zm, src, zxs, zc, zcx, zd, stat, y, rs_send, rs_recv, xs, xr, pk, un, s3, dyn, d3, zl, xfi, xfr, vacc, wrec, wear, warr,
    load_sem, in_sem, z_send, z_recv, rs_ssem, rs_rsem, x_ssem, x_rsem, s3_ssem, s3_rsem, d3_ssem, d3_rsem, i_ssem, i_rsem,
):
    me = lax.axis_index("row")
    sub = lax.axis_index("sub")
    last = steps - 1
    other = rows - ports
    xr2 = 2 * xfs
    prow = ports + xr2
    n_hop = n_row // 2

    def row_of(d):
        return lax.rem(me + d + 2 * n_row, n_row)

    def at_row(d):
        return (sub, row_of(d))

    def remote(a, b, ss, rs, dev):
        return pltpu.make_async_remote_copy(
            src_ref=a, dst_ref=b, send_sem=ss, recv_sem=rs, device_id=dev, device_id_type=MESH
        )

    def arrived(buf, rs):
        remote(buf, buf, rs, rs, at_row(1)).wait_recv()

    ld_ports = pltpu.make_async_copy(z.at[pl.ds(0, ports)], zm.at[pl.ds(0, ports)], load_sem.at[0])
    ld_rest = pltpu.make_async_copy(z.at[pl.ds(ports, other)], zm.at[pl.ds(ports, other)], load_sem.at[1])
    ld_src = pltpu.make_async_copy(source, src, load_sem.at[2])
    small = [
        pltpu.make_async_copy(a, b, in_sem.at[i])
        for i, (a, b) in enumerate(
            [
                (pattern_in, pattern), (xf_in, xf), (far_in, far), (delay_in, delay), (wave0_in, wave0),
                (flux0_in, flux0), (volt0_in, volt0), (slope_in, slope), (knee_in, knee),
            ]
        )
    ]
    small[0].start()
    ld_ports.start()
    barrier = pltpu.get_barrier_semaphore()

    def greet(i, c):
        pl.semaphore_signal(
            barrier, inc=1, device_id=(lax.rem(sub + i, n_sub), me), device_id_type=MESH
        )
        return c

    for d in range(1, n_row):
        pl.semaphore_signal(barrier, inc=1, device_id=at_row(d), device_id_type=MESH)
    lax.fori_loop(1, n_sub, greet, 0)
    ld_rest.start()
    ld_src.start()
    for cp in small[1:]:
        cp.start()

    def mask_rows(lo, count, brow):
        def one(b, c):
            m = jnp.where(pattern[brow, b] > 0, 1.0, 0.0).astype(F32)
            mv = jnp.full((1, block), m, F32).astype(BF)
            cols = pl.ds(pl.multiple_of(b * block, block), block)
            zm[lo : lo + count, cols] = zm[lo : lo + count, cols] * mv
            return c

        lax.fori_loop(0, n_row * rows // block, one, 0)

    small[0].wait()
    ld_ports.wait()
    mask_rows(0, ports, 0)

    pl.semaphore_wait(barrier, n_row - 1 + n_sub - 1)

    z_copies = []

    def send_ports(d):
        cols = pl.ds(pl.multiple_of(row_of(d) * rows, rows), rows)
        cp = remote(zm.at[pl.ds(0, ports), cols], zc.at[me, pl.ds(0, ports)], z_send.at[0, d], z_recv.at[0, d], at_row(d))
        cp.start()
        z_copies.append(cp)

    order = [n_hop]
    for d in range(n_hop - 1, 0, -1):
        order += [d, n_row - d]
    for d in order[:3]:
        send_ports(d)

    for cp in small[1:]:
        cp.wait()
    ri = lax.broadcasted_iota(jnp.int32, (xr2, rows), 0)
    li = lax.broadcasted_iota(jnp.int32, (xr2, rows), 1)
    oh = jnp.zeros((xr2, rows), F32)
    bi = lax.broadcasted_iota(jnp.int32, (xfs, 128), 0)
    lane = lax.broadcasted_iota(jnp.int32, (1, xfs), 1)
    idx = jnp.zeros((xfs, 128), jnp.int32)
    node_row = jnp.zeros((1, xfs), jnp.int32)
    for j in range(xfs):
        node = xf[0, j] & (rows - 1)
        oh = jnp.where((lax.rem(ri, xfs) == j) & (li == node), 1.0, oh)
        idx = jnp.where(bi == j, node, idx)
        node_row = jnp.where(lane == j, node, node_row)
    oh_cols = jnp.concatenate([oh, jnp.zeros((128 - xr2, rows), F32)], axis=0).astype(BF)
    oh = oh.astype(BF)
    xfi[...] = idx
    xfr[me] = idx
    shared = idx[:, 0:1] == node_row
    ahead = lax.broadcasted_iota(jnp.int32, (xfs, xfs), 1) < lax.broadcasted_iota(jnp.int32, (xfs, xfs), 0)
    first = jnp.sum(jnp.where(shared & ahead, 1, 0), axis=1, keepdims=True) == 0

    ld_rest.wait()
    mask_rows(ports, block - ports, 0)
    for b in range(1, rows // block):
        mask_rows(b * block, block, b)

    def pick(c, carry):
        cols = pl.ds(pl.multiple_of(c * rows, rows), rows)
        v = dot(oh, zm[0:rows, cols])
        zm[rows : rows + xr2, cols] = v.astype(BF)
        zxs[c] = jnp.concatenate([v[0:xfs, 0 : rows // 2], v[0:xfs, rows // 2 :]], axis=0).astype(BF)
        return carry

    lax.fori_loop(0, n_row, pick, 0)
    for d in order:
        cp = remote(zxs.at[row_of(d)], zcx.at[me], z_send.at[1, d], z_recv.at[1, d], at_row(d))
        cp.start()
        z_copies.append(cp)
        cp = remote(xfi, xfr.at[me], i_ssem.at[d], i_rsem.at[d], at_row(d))
        cp.start()
        z_copies.append(cp)
    for d in order[3:]:
        send_ports(d)

    eye = lax.broadcasted_iota(jnp.int32, (ports, ports), 0) == lax.broadcasted_iota(jnp.int32, (ports, ports), 1)
    before = lax.broadcasted_iota(jnp.int32, (ports, ports), 0) < lax.broadcasted_iota(jnp.int32, (ports, ports), 1)
    fs_row = far[0:1, :]
    fp_row = far[1:2, :]
    fs_col = jnp.sum(jnp.where(eye, fs_row, 0), axis=1, keepdims=True)
    fp_col = jnp.sum(jnp.where(eye, fp_row, 0), axis=1, keepdims=True)
    same = fs_col == fs_row
    rank_row = jnp.sum(jnp.where(same & before, 1, 0), axis=0, keepdims=True)
    rank_col = jnp.sum(jnp.where(same & (fp_row < fp_col), 1, 0), axis=1, keepdims=True)
    dl_col = jnp.sum(jnp.where(eye, delay[...], 0), axis=1, keepdims=True)
    late = dl_col == 2
    n_slot = 2 * SLOTS * n_sub
    place_row = fs_row * (2 * SLOTS) + rank_row
    place_col = fs_col * (2 * SLOTS) + rank_col
    for h in range(2):
        pi = lax.broadcasted_iota(jnp.int32, (n_slot, ports), 0)
        pk[:, h * ports : (h + 1) * ports] = jnp.where(pi == place_row + h * SLOTS, 1.0, 0.0).astype(BF)
        ui = lax.broadcasted_iota(jnp.int32, (ports, n_slot), 1)
        un[h * ports : (h + 1) * ports, :] = jnp.where(ui == place_col + h * SLOTS, 1.0, 0.0).astype(BF)
    own_slots = pl.ds(pl.multiple_of(sub * 2 * SLOTS, 2 * SLOTS), 2 * SLOTS)
    for t in range(last):
        xr[t, own_slots, :] = jnp.zeros((2 * SLOTS, HALF), BF)

    wrec[...] = wave0[0].astype(F32)
    wear[...] = wave0[1].astype(F32)
    dyn[...] = jnp.zeros_like(dyn)
    for c in range(n_row):
        d3[c, prow:] = jnp.zeros((d3.shape[1] - prow, d3.shape[2]), BF)

    def currents(flux, at_xf):
        total = slope[0] * flux
        for level in range(3):
            total = total + slope[level + 1] * (
                jnp.maximum(flux - knee[level], 0.0) + jnp.minimum(flux + knee[level], 0.0)
            )
        absorbed = jnp.zeros_like(total)
        for j in range(xfs):
            absorbed = absorbed + jnp.where(shared[:, j : j + 1], total[j : j + 1], 0.0)
        inject = (at_xf - absorbed).astype(BF).astype(F32)
        delta = jnp.where(first, inject - at_xf, 0.0)
        high = delta.astype(BF).astype(F32)
        return jnp.concatenate([high, delta - high], axis=0).astype(BF)

    ld_src.wait()
    at_xf = [dot(oh, src[t])[0:xfs] for t in range(steps)]

    def begin(t, flux):
        warr[...] = jnp.where(late, wear[...], wrec[...])
        cur = currents(flux, at_xf[t])
        if t < last:
            dyn[0:ports] = warr[...].astype(BF)
            dyn[ports:prow] = cur
        else:
            d3[me, 0:ports] = (src[last, 0:ports, :].astype(F32) + warr[...]).astype(BF)
            d3[me, ports:prow] = cur

    flux = flux0[...]
    xprev = volt0[...]
    begin(0, flux)

    zc[me, 0:ports] = zm[0:ports, pl.ds(pl.multiple_of(me * rows, rows), rows)]
    zcx[me] = zxs[me]
    s3[me] = src[last, ports:rows, :]

    def products(r):
        v = zcx[r].astype(F32)
        v = jnp.concatenate([v[0:xfs], v[xfs:]], axis=1)
        zc[r, ports:prow] = jnp.concatenate([v, jnp.zeros_like(v)], axis=0).astype(BF)
        zr = zc[r]
        zd[r, :, 0:ports] = zc[r, :, 0:ports]
        zd[r, :, ports:] = dot_t(zr, oh_cols).astype(BF)
        y[r] = dot(zr, src[0]) + dot(zd[r], dyn[...])
        for t in range(1, last):
            stat[t - 1, r] = dot(zr, src[t])

    def add_dynamic(t, r):
        y[r] = stat[t - 1, r] + dot(zd[r], dyn[...])

    first_dir = jnp.where(lax.rem(me, n_hop) < n_hop // 2, 1, 0)

    def both_ways(f):
        for j in range(2):
            dirn = jnp.bitwise_xor(first_dir, j)
            f(dirn, 1 - 2 * dirn)

    def both(v):
        v = v.astype(F32)
        return v[0:xfs] + v[xfs:]

    sends = []

    def reduce_scatter(t, ready):
        def push(dirn, dest, slot, h, to, got):
            lanes = pl.ds(pl.multiple_of(h * HALF, HALF), HALF)
            acc_p = y[dest, 0:ports, lanes]
            acc_x = y[dest, ports : ports + xfs, lanes]
            for g in got:
                buf = rs_recv.at[t, dirn, g, h]
                arrived(buf, rs_rsem.at[t, dirn, g, h])
                acc_p = acc_p + buf[0:ports].astype(F32)
                acc_x = acc_x + both(buf[ports:prow])
            high = acc_x.astype(BF).astype(F32)
            rs_send[t, dirn, slot, h, 0:ports] = acc_p.astype(BF)
            rs_send[t, dirn, slot, h, ports:prow] = jnp.concatenate([high, acc_x - high], axis=0).astype(BF)
            cp = remote(
                rs_send.at[t, dirn, slot, h], rs_recv.at[t, dirn, slot, h],
                rs_ssem.at[t, dirn, slot, h], rs_rsem.at[t, dirn, slot, h], at_row(to),
            )
            cp.start()
            sends.append(cp)

        ready(4)
        both_ways(lambda dirn, sign: push(dirn, row_of(4 * sign), 0, dirn, 2 * sign, ()))
        ready(3)

        def second(dirn, sign):
            for h in range(2):
                push(dirn, row_of(3 * sign), 1, h, sign, ())

        both_ways(second)
        ready(2)

        def third(dirn, sign):
            push(dirn, row_of(2 * sign), 2, 1 - dirn, sign, (1,))
            push(dirn, row_of(2 * sign), 2, dirn, sign, (0, 1))

        both_ways(third)
        ready(1)

        def fourth(dirn, sign):
            for h in (1 - dirn, dirn):
                push(dirn, row_of(sign), 3, h, sign, (2,))

        both_ways(fourth)
        ready(0)
        at_ports, at_xfs = [], []
        for h in range(2):
            lanes = slice(h * HALF, (h + 1) * HALF)
            for dirn in range(2):
                arrived(rs_recv.at[t, dirn, 3, h], rs_rsem.at[t, dirn, 3, h])
            left, right = rs_recv.at[t, 0, 3, h], rs_recv.at[t, 1, 3, h]
            at_ports.append(y[me, 0:ports, lanes] + left[0:ports].astype(F32) + right[0:ports].astype(F32))
            at_xfs.append(y[me, ports : ports + xfs, lanes] + both(left[ports:prow]) + both(right[ports:prow]))
        return at_ports, at_xfs

    s3_cut = other // 2

    def s3_hop(k):
        for dirn in range(2):
            sign = 1 - 2 * dirn
            c = row_of(-sign * k)
            if k < n_hop - 1:
                part = pl.ds(0, other)
            else:
                part = pl.ds(dirn * s3_cut, s3_cut)
            cp = remote(s3.at[c, part], s3.at[c, part], s3_ssem.at[dirn, k], s3_rsem.at[dirn, k], at_row(sign))
            cp.start()
            sends.append(cp)

    def s3_wait(k):
        for dirn in range(2):
            part = pl.ds(0, other) if k < n_hop - 1 else pl.ds(0, s3_cut)
            arrived(s3.at[me, part], s3_rsem.at[dirn, k])

    def add_static(c):
        lo = pl.multiple_of(c * rows + ports, ports)
        vacc[...] += dot(zm[:, pl.ds(lo, other)], s3[c])

    def add_last(c):
        vacc[...] += dot(zl[c], d3[c])

    def columns(c, carry):
        node = xfr[c][:, 0:1]
        hot = jnp.where(lax.broadcasted_iota(jnp.int32, (xfs, rows), 1) == node, 1.0, 0.0)
        hot = jnp.concatenate([hot, hot, jnp.zeros((128 - xr2, rows), F32)], axis=0).astype(BF)
        zl[c, :, 0:ports] = zm[:, pl.ds(pl.multiple_of(c * rows, rows), ports)]
        zl[c, :, ports:] = dot_t(zm[:, pl.ds(pl.multiple_of(c * rows, rows), rows)], hot).astype(BF)
        return carry

    products(me)
    vacc[...] = jnp.zeros_like(vacc)
    add_static(me)
    for d in range(1, n_row):
        arrived(xfr.at[row_of(-d)], i_rsem.at[d])
    lax.fori_loop(0, n_row, columns, 0)

    for t in range(last):

        def ready(d, t=t):
            for e in (d, n_row - d) if 0 < d < n_hop else (d,):
                r = row_of(e)
                if t:
                    add_dynamic(t, r)
                elif e:
                    arrived(zc.at[r, pl.ds(0, ports)], z_recv.at[0, n_row - e])
                    arrived(zcx.at[r], z_recv.at[1, n_row - e])
                    products(r)

        at_ports, at_xfs = reduce_scatter(t, ready)
        xv = jnp.concatenate(at_xfs, axis=1)
        flux = flux + 0.5 * (xv + xprev)
        xprev = xv
        out = jnp.concatenate(
            [0.5 * at_ports[h] - warr[:, h * HALF : (h + 1) * HALF] for h in range(2)], axis=0
        ).astype(BF)
        xs[t] = dot(pk[...], out).astype(BF)

        def put(i, c, t=t):
            p = lax.rem(sub + i, n_sub)
            remote(
                xs.at[t, pl.ds(pl.multiple_of(p * 2 * SLOTS, 2 * SLOTS), 2 * SLOTS)],
                xr.at[t, own_slots],
                x_ssem.at[t],
                x_rsem.at[t],
                (p, me),
            ).start()
            return c

        lax.fori_loop(1, n_sub, put, 0)
        if t:
            s3_wait(t - 1)
        s3_hop(t)
        if t:
            add_static(row_of(-t))
            add_static(row_of(t))
        total = pl.ds(0, (n_sub - 1) * 2 * SLOTS)
        pltpu.make_async_copy(xs.at[t, total], xr.at[t, total], x_rsem.at[t]).wait()
        inc = dot(un[...], xr[t])
        wear[...] = wrec[...]
        wrec[...] = jnp.concatenate([inc[0:ports], inc[ports : 2 * ports]], axis=1)
        begin(t + 1, flux)

    parts = ((0, ports // 2), (ports // 2, prow - ports // 2))

    def d3_send(dirn, sign, slot, p, c, to):
        part = pl.ds(*parts[p])
        cp = remote(d3.at[c, part], d3.at[c, part], d3_ssem.at[dirn, slot, p], d3_rsem.at[dirn, slot, p], at_row(to))
        cp.start()
        sends.append(cp)

    def d3_wait(dirn, slot, p):
        arrived(d3.at[me, pl.ds(*parts[p])], d3_rsem.at[dirn, slot, p])

    for p in range(2):
        both_ways(lambda dirn, sign: d3_send(dirn, sign, 0, p, me, sign))
    add_last(me)
    s3_wait(n_hop - 2)
    s3_hop(n_hop - 1)
    for k in (1, 2):

        def forward(dirn, sign):
            for p in range(2):
                d3_wait(dirn, k - 1, p)
                d3_send(dirn, sign, k, p, row_of(-sign * k), sign)
                if k == 2:
                    @pl.when(dirn == p)
                    def _():
                        part = pl.ds(*parts[p])
                        c = row_of(-sign * k)
                        remote(
                            d3.at[c, part], d3.at[c, part], d3_ssem.at[dirn, 3, p], d3_rsem.at[dirn, 3, p], at_row(2 * sign)
                        ).start()

        both_ways(forward)
        add_last(row_of(-k))
        add_last(row_of(k))
        if k == 1:
            add_static(row_of(-(n_hop - 1)))
            add_static(row_of(n_hop - 1))
    s3_wait(n_hop - 1)
    add_static(row_of(n_hop))
    for p in range(2):
        both_ways(lambda dirn, sign: d3_wait(dirn, 2, p))
    add_last(row_of(-3))
    add_last(row_of(3))
    for p in range(2):
        d3_wait(p, 3, p)
    add_last(row_of(n_hop))
    out_copy = pltpu.make_async_copy(vacc.at[pl.ds(0, rows)], vout, load_sem.at[0])
    out_copy.start()
    flux0[...] = flux + 0.5 * (vacc[rows : rows + xfs] + xprev)
    flux_copy = pltpu.make_async_copy(flux0, fout, load_sem.at[1])
    flux_copy.start()

    for cp in z_copies + sends:
        cp.wait_send()
    for p in range(2):
        buf = d3.at[me, pl.ds(*parts[p])]
        remote(buf, buf, d3_ssem.at[p, 3, p], d3_rsem.at[p, 3, p], at_row(1)).wait_send()
    for t in range(last):
        total = pl.ds(0, (n_sub - 1) * 2 * SLOTS)
        pltpu.make_async_copy(xs.at[t, total], xr.at[t, total], x_ssem.at[t]).wait()
    out_copy.wait()
    flux_copy.wait()


def body(source, inverse_z, pattern, line_far, delay, xf_node, wave0, flux0, volt0, slope, knee):
    steps, _, rows, scen = source.shape
    nodes = inverse_z.shape[2]
    ports = line_far.shape[1]
    xfs = xf_node.shape[1]
    n_sub, n_row = lax.axis_size("sub"), lax.axis_size("row")
    block = nodes // pattern.shape[2]
    last = steps - 1
    xr2 = 2 * xfs
    prow = ports + xr2
    n_hop = n_row // 2
    other = rows - ports
    n_slot = 2 * SLOTS * n_sub
    hbm = pl.BlockSpec(memory_space=pltpu.HBM)
    dma = pltpu.SemaphoreType.DMA
    voltage, flux = pl.pallas_call(
        functools.partial(kernel, n_sub, n_row, rows, ports, xfs, steps, block),
        out_shape=(
            jax.ShapeDtypeStruct((rows, scen), F32),
            jax.ShapeDtypeStruct((xfs, scen), F32),
        ),
        in_specs=[hbm] * 11,
        out_specs=(hbm, hbm),
        scratch_shapes=[
            pltpu.SMEM(pattern.shape[1:], jnp.int32),
            pltpu.VMEM((2, ports), jnp.int32),
            pltpu.VMEM(delay.shape, jnp.int32),
            pltpu.SMEM(xf_node.shape, jnp.int32),
            pltpu.VMEM((2, ports, scen), BF),
            pltpu.VMEM((xfs, scen), F32),
            pltpu.VMEM((xfs, scen), F32),
            pltpu.SMEM(slope.shape, F32),
            pltpu.SMEM(knee.shape, F32),
            pltpu.VMEM((rows + xr2, nodes), BF),
            pltpu.VMEM((steps, rows, scen), BF),
            pltpu.VMEM((n_row, xr2, rows // 2), BF),
            pltpu.VMEM((n_row, prow, rows), BF),
            pltpu.VMEM((n_row, xr2, rows // 2), BF),
            pltpu.VMEM((n_row, prow, ports + 128), BF),
            pltpu.VMEM((last - 1, n_row, prow, scen), F32),
            pltpu.VMEM((n_row, prow, scen), F32),
            pltpu.VMEM((last, 2, 4, 2, prow, HALF), BF),
            pltpu.VMEM((last, 2, 4, 2, prow, HALF), BF),
            pltpu.VMEM((last, n_slot, HALF), BF),
            pltpu.VMEM((last, n_slot, HALF), BF),
            pltpu.VMEM((n_slot, 2 * ports), BF),
            pltpu.VMEM((2 * ports, n_slot), BF),
            pltpu.VMEM((n_row, other, scen), BF),
            pltpu.VMEM((ports + 128, scen), BF),
            pltpu.VMEM((n_row, ports + 128, scen), BF),
            pltpu.VMEM((n_row, rows + xr2, ports + 128), BF),
            pltpu.VMEM((xfs, 128), jnp.int32),
            pltpu.VMEM((n_row, xfs, 128), jnp.int32),
            pltpu.VMEM((rows + xr2, scen), F32),
            pltpu.VMEM((ports, scen), F32),
            pltpu.VMEM((ports, scen), F32),
            pltpu.VMEM((ports, scen), F32),
            dma((3,)),
            dma((9,)),
            dma((2, n_row)),
            dma((2, n_row)),
            dma((last, 2, 4, 2)),
            dma((last, 2, 4, 2)),
            dma((last,)),
            dma((last,)),
            dma((2, n_hop)),
            dma((2, n_hop)),
            dma((2, 4, 2)),
            dma((2, 4, 2)),
            dma((n_row,)),
            dma((n_row,)),
        ],
        compiler_params=pltpu.CompilerParams(
            collective_id=0, has_side_effects=True, vmem_limit_bytes=63 * 2**20
        ),
        name="grid_steps",
    )(
        source.reshape(steps, rows, scen),
        inverse_z.reshape(rows, nodes),
        pattern.reshape(pattern.shape[1:]),
        jnp.swapaxes(line_far.reshape(ports, 2), 0, 1),
        delay,
        xf_node,
        wave0.reshape(2, ports, scen),
        flux0.reshape(xfs, scen),
        volt0.reshape(xfs, scen),
        slope,
        knee,
    )
    return (voltage[None], flux[None])


def solution(mesh):
    return jax.shard_map(
        body,
        mesh=mesh,
        in_specs=(
            P(None, "sub", "row", None),
            P("sub", "row", None),
            P("sub", "row", None),
            P("sub", "row", None),
            P("sub", "row"),
            P("sub", "row"),
            P(None, "sub", "row", None),
            P("sub", "row", None),
            P("sub", "row", None),
            P(),
            P(),
        ),
        out_specs=(P("sub", "row", None), P("sub", "row", None)),
        check_vma=False,
    )
```

time: 125 us -> 107 us (0.86)
  Pallas kernels: 113 us -> 103 us
  local copies, waits for them, and re-layouts: 11.2 us -> 3.16 us
    pallas_call x1, Pallas kernels: 113 us -> 103 us  [body(): pl.pallas_call(functools.partial(kernel, n_sub, n_row, rows, ports, xfs,...]
    unnamed x23 -> x2, local copies, waits for them, and re-layouts: 11.2 us -> 3.16 us
where the time goes in v2:
time: 107 us
  Pallas kernels  103 us (96%)
  local copies, waits for them, and re-layouts  3.16 us (3%)
    pallas_call x1, Pallas kernels, body(): pl.pallas_call(functools.partial(kernel, n_sub, n_row, rows, ports, xfs,...  103 us
    unnamed x2, local copies, waits for them, and re-layouts  3.16 us

profile of v2, /device:TPU:2, one launch (start us, length us, event | category | flops | bytes accessed | tf_op | source)
XLA Modules:
  0.0 106.6 jit_solution(18004115495669278304)
XLA Ops:
  0.6 102.7 %grid_steps.1 = (f32[512,256]{1,0:T(8,128)}, f32[8,256]{1,0:T(8,128)}) custom-call(bf16[4,512,256]{2,1,0:T(8,128)(2,1)} %bitcast.12, bf16[512,4096]{1,0:T(8,128)(2,1)} %bitcast.11, s32[2,16]{1,0:T(2,128)} %bitcast.18, s32[2,128]{1,0:T(2,128)} %bitcast.19, s32[1,128]{1,0:T(1,128)} %delay_in.1, s32[1,8]{1,0:T(1,128)} %xf_in.1, bf16[2,128,256]{2,1,0:T(8,128)(2,1)} %bitcast.14, ...), custom_call_target="tpu_custom_call" | custom-call | tf_op jit(solution)/shard_map/grid_steps/pallas_call | solution.py:471
  103.4 1.9 %copy.15 = f32[1,512,256]{2,1,0:T(8,128)} copy(f32[1,512,256]{2,1,0:T(8,128)} %bitcast.13) | data formatting | bytes 1048576
  105.3 1.3 %copy.16 = f32[1,8,256]{2,1,0:T(8,128)} copy(f32[1,8,256]{2,1,0:T(8,128)} %bitcast.17) | data formatting | bytes 16384

commit v3 on v2

--- a/solution.py
+++ b/solution.py
@@ -52,9 +52,16 @@
     def arrived(buf, rs):
         remote(buf, buf, rs, rs, at_row(1)).wait_recv()
 
-    ld_ports = pltpu.make_async_copy(z.at[pl.ds(0, ports)], zm.at[pl.ds(0, ports)], load_sem.at[0])
-    ld_rest = pltpu.make_async_copy(z.at[pl.ds(ports, other)], zm.at[pl.ds(ports, other)], load_sem.at[1])
-    ld_src = pltpu.make_async_copy(source, src, load_sem.at[2])
+    peers = sorted(range(1, n_sub), key=lambda i: -sum((0, 1, 2, 1)[(i >> b) & 3] for b in range(1, n_sub.bit_length(), 2)))
+    order = []
+    for d in range(n_hop - 1, 0, -1):
+        order += [d, n_row - d] + ([n_hop] if d == n_hop - 1 else [])
+
+    def peer(i):
+        return jnp.bitwise_xor(sub, i)
+
+    ld_z = pltpu.make_async_copy(z, zm.at[pl.ds(0, rows)], load_sem.at[0])
+    ld_src = pltpu.make_async_copy(source, src, load_sem.at[1])
     small = [
         pltpu.make_async_copy(a, b, in_sem.at[i])
         for i, (a, b) in enumerate(
@@ -64,80 +71,79 @@
             ]
         )
     ]
-    small[0].start()
-    ld_ports.start()
     barrier = pltpu.get_barrier_semaphore()
-
-    def greet(i, c):
-        pl.semaphore_signal(
-            barrier, inc=1, device_id=(lax.rem(sub + i, n_sub), me), device_id_type=MESH
-        )
-        return c
-
-    for d in range(1, n_row):
+    for i in peers:
+        pl.semaphore_signal(barrier, inc=1, device_id=(peer(i), me), device_id_type=MESH)
+    for d in order:
         pl.semaphore_signal(barrier, inc=1, device_id=at_row(d), device_id_type=MESH)
-    lax.fori_loop(1, n_sub, greet, 0)
-    ld_rest.start()
+    for cp in small[:2]:
+        cp.start()
+    ld_z.start()
     ld_src.start()
-    for cp in small[1:]:
+    for cp in small[2:]:
         cp.start()
 
-    def mask_rows(lo, count, brow):
-        def one(b, c):
-            m = jnp.where(pattern[brow, b] > 0, 1.0, 0.0).astype(F32)
-            mv = jnp.full((1, block), m, F32).astype(BF)
-            cols = pl.ds(pl.multiple_of(b * block, block), block)
-            zm[lo : lo + count, cols] = zm[lo : lo + count, cols] * mv
-            return c
-
-        lax.fori_loop(0, n_row * rows // block, one, 0)
-
-    small[0].wait()
-    ld_ports.wait()
-    mask_rows(0, ports, 0)
+    for cp in small[:2]:
+        cp.wait()
+    bi = lax.broadcasted_iota(jnp.int32, (2 * xfs, 128), 0)
+    idx = jnp.zeros((2 * xfs, 128), jnp.int32)
+    for j in range(xfs):
+        idx = jnp.where(bi == j, xf[0, j] & (rows - 1), idx)
+    for c in range(n_row):
+        v = idx
+        for b in range(rows // block):
+            v = jnp.where(bi == xfs + b, pattern[0, c * (rows // block) + b], v)
+        xfi[c] = v
 
     pl.semaphore_wait(barrier, n_row - 1 + n_sub - 1)
 
     z_copies = []
-
-    def send_ports(d):
+    port_copies = []
+    tail = list(order)
+
+    def next_ports():
+        if len(port_copies) >= 3:
+            port_copies[-3].wait_send()
+        d = tail.pop(0)
         cols = pl.ds(pl.multiple_of(row_of(d) * rows, rows), rows)
-        cp = remote(zm.at[pl.ds(0, ports), cols], zc.at[me, pl.ds(0, ports)], z_send.at[0, d], z_recv.at[0, d], at_row(d))
+        cp = remote(z.at[pl.ds(0, ports), cols], zc.at[me, pl.ds(0, ports)], z_send.at[0, d], z_recv.at[0, d], at_row(d))
+        cp.start()
+        port_copies.append(cp)
+
+    for d in order:
+        cp = remote(xfi.at[row_of(d)], xfr.at[me], i_ssem.at[d], i_rsem.at[d], at_row(d))
         cp.start()
         z_copies.append(cp)
-
-    order = [n_hop]
-    for d in range(n_hop - 1, 0, -1):
-        order += [d, n_row - d]
-    for d in order[:3]:
-        send_ports(d)
-
-    for cp in small[1:]:
-        cp.wait()
+    for _ in range(3):
+        next_ports()
+    xfr[me] = xfi[me]
+
     ri = lax.broadcasted_iota(jnp.int32, (xr2, rows), 0)
     li = lax.broadcasted_iota(jnp.int32, (xr2, rows), 1)
     oh = jnp.zeros((xr2, rows), F32)
-    bi = lax.broadcasted_iota(jnp.int32, (xfs, 128), 0)
     lane = lax.broadcasted_iota(jnp.int32, (1, xfs), 1)
-    idx = jnp.zeros((xfs, 128), jnp.int32)
     node_row = jnp.zeros((1, xfs), jnp.int32)
     for j in range(xfs):
         node = xf[0, j] & (rows - 1)
         oh = jnp.where((lax.rem(ri, xfs) == j) & (li == node), 1.0, oh)
-        idx = jnp.where(bi == j, node, idx)
         node_row = jnp.where(lane == j, node, node_row)
     oh_cols = jnp.concatenate([oh, jnp.zeros((128 - xr2, rows), F32)], axis=0).astype(BF)
     oh = oh.astype(BF)
-    xfi[...] = idx
-    xfr[me] = idx
-    shared = idx[:, 0:1] == node_row
+    shared = idx[0:xfs, 0:1] == node_row
     ahead = lax.broadcasted_iota(jnp.int32, (xfs, xfs), 1) < lax.broadcasted_iota(jnp.int32, (xfs, xfs), 0)
     first = jnp.sum(jnp.where(shared & ahead, 1, 0), axis=1, keepdims=True) == 0
 
-    ld_rest.wait()
-    mask_rows(ports, block - ports, 0)
-    for b in range(1, rows // block):
-        mask_rows(b * block, block, b)
+    ld_z.wait()
+    for brow in range(rows // block):
+
+        def mask(b, c, brow=brow):
+            m = jnp.where(pattern[brow, b] > 0, 1.0, 0.0).astype(F32)
+            mv = jnp.full((1, block), m, F32).astype(BF)
+            at = (pl.ds(brow * block, block), pl.ds(pl.multiple_of(b * block, block), block))
+            zm[at] = zm[at] * mv
+            return c
+
+        lax.fori_loop(0, n_row * rows // block, mask, 0)
 
     def pick(c, carry):
         cols = pl.ds(pl.multiple_of(c * rows, rows), rows)
@@ -151,12 +157,9 @@
         cp = remote(zxs.at[row_of(d)], zcx.at[me], z_send.at[1, d], z_recv.at[1, d], at_row(d))
         cp.start()
         z_copies.append(cp)
-        cp = remote(xfi, xfr.at[me], i_ssem.at[d], i_rsem.at[d], at_row(d))
-        cp.start()
-        z_copies.append(cp)
-    for d in order[3:]:
-        send_ports(d)
-
+
+    for cp in small[2:]:
+        cp.wait()
     eye = lax.broadcasted_iota(jnp.int32, (ports, ports), 0) == lax.broadcasted_iota(jnp.int32, (ports, ports), 1)
     before = lax.broadcasted_iota(jnp.int32, (ports, ports), 0) < lax.broadcasted_iota(jnp.int32, (ports, ports), 1)
     fs_row = far[0:1, :]
@@ -225,6 +228,9 @@
         v = zcx[r].astype(F32)
         v = jnp.concatenate([v[0:xfs], v[xfs:]], axis=1)
         zc[r, ports:prow] = jnp.concatenate([v, jnp.zeros_like(v)], axis=0).astype(BF)
+        keep = [jnp.where(xfr[r, xfs + b : xfs + b + 1] > 0, 1.0, 0.0) for b in range(rows // block)]
+        keep = jnp.concatenate([k for k in keep for _ in range(block // 128)], axis=1).astype(BF)
+        zc[r, 0:ports] = zc[r, 0:ports] * keep
         zr = zc[r]
         zd[r, :, 0:ports] = zc[r, :, 0:ports]
         zd[r, :, ports:] = dot_t(zr, oh_cols).astype(BF)
@@ -329,7 +335,7 @@
         vacc[...] += dot(zl[c], d3[c])
 
     def columns(c, carry):
-        node = xfr[c][:, 0:1]
+        node = xfr[c, 0:xfs, 0:1]
         hot = jnp.where(lax.broadcasted_iota(jnp.int32, (xfs, rows), 1) == node, 1.0, 0.0)
         hot = jnp.concatenate([hot, hot, jnp.zeros((128 - xr2, rows), F32)], axis=0).astype(BF)
         zl[c, :, 0:ports] = zm[:, pl.ds(pl.multiple_of(c * rows, rows), ports)]
@@ -346,6 +352,12 @@
     for t in range(last):
 
         def ready(d, t=t):
+            if t == 0 and d == n_hop:
+                for _ in range(2):
+                    next_ports()
+            if t == 0 and d == n_hop - 2:
+                for _ in range(2):
+                    next_ports()
             for e in (d, n_row - d) if 0 < d < n_hop else (d,):
                 r = row_of(e)
                 if t:
@@ -363,9 +375,8 @@
             [0.5 * at_ports[h] - warr[:, h * HALF : (h + 1) * HALF] for h in range(2)], axis=0
         ).astype(BF)
         xs[t] = dot(pk[...], out).astype(BF)
-
-        def put(i, c, t=t):
-            p = lax.rem(sub + i, n_sub)
+        for i in peers:
+            p = peer(i)
             remote(
                 xs.at[t, pl.ds(pl.multiple_of(p * 2 * SLOTS, 2 * SLOTS), 2 * SLOTS)],
                 xr.at[t, own_slots],
@@ -373,9 +384,6 @@
                 x_rsem.at[t],
                 (p, me),
             ).start()
-            return c
-
-        lax.fori_loop(1, n_sub, put, 0)
         if t:
             s3_wait(t - 1)
         s3_hop(t)
@@ -441,7 +449,7 @@
     flux_copy = pltpu.make_async_copy(flux0, fout, load_sem.at[1])
     flux_copy.start()
 
-    for cp in z_copies + sends:
+    for cp in z_copies + port_copies[-3:] + sends:
         cp.wait_send()
     for p in range(2):
         buf = d3.at[me, pl.ds(*parts[p])]
@@ -451,6 +459,11 @@
         pltpu.make_async_copy(xs.at[t, total], xr.at[t, total], x_ssem.at[t]).wait()
     out_copy.wait()
     flux_copy.wait()
+
+
+def hand_over(acc, flux_in, vout, fout):
+    vout[...] = acc[...]
+    fout[...] = flux_in[...]
 
 
 def body(source, inverse_z, pattern, line_far, delay, xf_node, wave0, flux0, volt0, slope, knee):
@@ -504,13 +517,13 @@
             pltpu.VMEM((ports + 128, scen), BF),
             pltpu.VMEM((n_row, ports + 128, scen), BF),
             pltpu.VMEM((n_row, rows + xr2, ports + 128), BF),
-            pltpu.VMEM((xfs, 128), jnp.int32),
-            pltpu.VMEM((n_row, xfs, 128), jnp.int32),
+            pltpu.VMEM((n_row, 2 * xfs, 128), jnp.int32),
+            pltpu.VMEM((n_row, 2 * xfs, 128), jnp.int32),
             pltpu.VMEM((rows + xr2, scen), F32),
             pltpu.VMEM((ports, scen), F32),
             pltpu.VMEM((ports, scen), F32),
             pltpu.VMEM((ports, scen), F32),
-            dma((3,)),
+            dma((2,)),
             dma((9,)),
             dma((2, n_row)),
             dma((2, n_row)),
@@ -542,6 +555,18 @@
         slope,
         knee,
     )
+    vmem = pl.BlockSpec(memory_space=pltpu.VMEM)
+    voltage, flux = pl.pallas_call(
+        hand_over,
+        out_shape=(
+            jax.ShapeDtypeStruct((rows, scen), F32),
+            jax.ShapeDtypeStruct((xfs, scen), F32),
+        ),
+        in_specs=[vmem] * 2,
+        out_specs=(vmem, vmem),
+        compiler_params=pltpu.CompilerParams(vmem_limit_bytes=63 * 2**20),
+        name="hand_over",
+    )(voltage, flux)
     return (voltage[None], flux[None])
 
 

time: 107 us -> 104 us (0.972)
  local copies, waits for them, and re-layouts: 3.16 us -> 0 us
    unnamed x2 -> x0, local copies, waits for them, and re-layouts: 3.16 us -> none
    pallas_call x1, Pallas kernels: 103 us -> 101 us  [body(): pl.pallas_call(functools.partial(kernel, n_sub, n_row, rows, ports, xfs,...]
    pallas_call x0 -> x1, Pallas kernels: none -> 1.87 us  [body(): pl.pallas_call(hand_over, out_shape=(jax.ShapeDtypeStruct((rows, scen), F...]
where the time goes in v3:
time: 104 us; the launch traced here: 103 us
  Pallas kernels  102 us (98%)
    pallas_call x1, Pallas kernels, body(): pl.pallas_call(functools.partial(kernel, n_sub, n_row, rows, ports, xfs,...  101 us

profile of v3, /device:TPU:2, one launch (start us, length us, event | category | flops | bytes accessed | tf_op | source)
XLA Modules:
  0.0 103.0 jit_solution(4399386784312031800)
XLA Ops:
  0.6 100.5 %grid_steps.1 = (f32[512,256]{1,0:T(8,128)}, f32[8,256]{1,0:T(8,128)}) custom-call(bf16[4,512,256]{2,1,0:T(8,128)(2,1)} %bitcast.12, bf16[512,4096]{1,0:T(8,128)(2,1)} %bitcast.11, s32[2,16]{1,0:T(2,128)} %bitcast.16, s32[2,128]{1,0:T(2,128)} %bitcast.17, s32[1,128]{1,0:T(1,128)} %delay_in.1, s32[1,8]{1,0:T(1,128)} %xf_in.1, bf16[2,128,256]{2,1,0:T(8,128)(2,1)} %bitcast.13, ...), custom_call_target="tpu_custom_call" | custom-call | tf_op jit(solution)/shard_map/grid_steps/pallas_call | solution.py:484
  101.2 1.9 %hand_over.1 = (f32[512,256]{1,0:T(8,128)}, f32[8,256]{1,0:T(8,128)}) custom-call(f32[512,256]{1,0:T(8,128)} %get-tuple-element.6.acc, f32[8,256]{1,0:T(8,128)} %get-tuple-element.7.flux_in), custom_call_target="tpu_custom_call" | custom-call | tf_op jit(solution)/shard_map/hand_over/pallas_call | solution.py:559

commit v4 on v3

--- a/solution.py
+++ b/solution.py
@@ -224,22 +224,35 @@
     zcx[me] = zxs[me]
     s3[me] = src[last, ports:rows, :]
 
-    def products(r):
+    places = [n_hop]
+    for d in range(n_hop - 1, 0, -1):
+        places += [d, n_row - d]
+    places += [0]
+
+    def block_at(i):
+        return pl.ds(pl.multiple_of(i * prow, 16), prow)
+
+    def products(i):
+        r = row_of(places[i])
+        keep = [jnp.where(xfr[r, xfs + b : xfs + b + 1] > 0, 1.0, 0.0) for b in range(rows // block)]
+        keep = jnp.concatenate([k for k in keep for _ in range(block // 128)], axis=1).astype(BF)
+        zc[r, 0:ports] = zc[r, 0:ports] * keep
         v = zcx[r].astype(F32)
         v = jnp.concatenate([v[0:xfs], v[xfs:]], axis=1)
         zc[r, ports:prow] = jnp.concatenate([v, jnp.zeros_like(v)], axis=0).astype(BF)
-        keep = [jnp.where(xfr[r, xfs + b : xfs + b + 1] > 0, 1.0, 0.0) for b in range(rows // block)]
-        keep = jnp.concatenate([k for k in keep for _ in range(block // 128)], axis=1).astype(BF)
-        zc[r, 0:ports] = zc[r, 0:ports] * keep
         zr = zc[r]
-        zd[r, :, 0:ports] = zc[r, :, 0:ports]
-        zd[r, :, ports:] = dot_t(zr, oh_cols).astype(BF)
-        y[r] = dot(zr, src[0]) + dot(zd[r], dyn[...])
+        zd[block_at(i), 0:ports] = zc[r, :, 0:ports]
+        zd[block_at(i), ports:] = dot_t(zr, oh_cols).astype(BF)
+        y[block_at(i)] = dot(zr, src[0]) + dot(zd[block_at(i)], dyn[...])
+
+    def static_products(i):
+        zr = zc[row_of(places[i])]
         for t in range(1, last):
-            stat[t - 1, r] = dot(zr, src[t])
-
-    def add_dynamic(t, r):
-        y[r] = stat[t - 1, r] + dot(zd[r], dyn[...])
+            stat[t - 1, block_at(i)] = dot(zr, src[t])
+
+    def add_dynamic(t, lo, hi):
+        at = pl.ds(lo * prow, (hi - lo) * prow)
+        y[at] = stat[t - 1, at] + dot(zd[at], dyn[...])
 
     first_dir = jnp.where(lax.rem(me, n_hop) < n_hop // 2, 1, 0)
 
@@ -255,10 +268,12 @@
     sends = []
 
     def reduce_scatter(t, ready):
-        def push(dirn, dest, slot, h, to, got):
+        def push(dirn, k, slot, h, to, got):
             lanes = pl.ds(pl.multiple_of(h * HALF, HALF), HALF)
-            acc_p = y[dest, 0:ports, lanes]
-            acc_x = y[dest, ports : ports + xfs, lanes]
+            place = 0 if k == n_hop else 1 + 2 * (n_hop - 1 - k) + dirn
+            lo = pl.multiple_of(place * prow, 16)
+            acc_p = y[pl.ds(lo, ports), lanes]
+            acc_x = y[pl.ds(pl.multiple_of(lo + ports, 16), xfs), lanes]
             for g in got:
                 buf = rs_recv.at[t, dirn, g, h]
                 arrived(buf, rs_rsem.at[t, dirn, g, h])
@@ -274,38 +289,45 @@
             cp.start()
             sends.append(cp)
 
-        ready(4)
-        both_ways(lambda dirn, sign: push(dirn, row_of(4 * sign), 0, dirn, 2 * sign, ()))
-        ready(3)
+        far_to = 2
+
+        def first_leg(dirn, sign):
+            push(dirn, 4, 0, dirn, far_to * sign, ())
 
         def second(dirn, sign):
-            for h in range(2):
-                push(dirn, row_of(3 * sign), 1, h, sign, ())
-
+            if far_to == 1:
+                push(dirn, 3, 1, 1 - dirn, sign, ())
+                push(dirn, 3, 1, dirn, sign, (0,))
+            else:
+                for h in range(2):
+                    push(dirn, 3, 1, h, sign, ())
+
+        def third(dirn, sign):
+            push(dirn, 2, 2, 1 - dirn, sign, (1,))
+            push(dirn, 2, 2, dirn, sign, (1,) if far_to == 1 else (0, 1))
+
+        def fourth(dirn, sign):
+            for h in (1 - dirn, dirn):
+                push(dirn, 1, 3, h, sign, (2,))
+
+        ready(0)
+        both_ways(first_leg)
+        ready(1)
         both_ways(second)
         ready(2)
-
-        def third(dirn, sign):
-            push(dirn, row_of(2 * sign), 2, 1 - dirn, sign, (1,))
-            push(dirn, row_of(2 * sign), 2, dirn, sign, (0, 1))
-
         both_ways(third)
-        ready(1)
-
-        def fourth(dirn, sign):
-            for h in (1 - dirn, dirn):
-                push(dirn, row_of(sign), 3, h, sign, (2,))
-
+        ready(3)
         both_ways(fourth)
-        ready(0)
+        ready(4)
+        own = (n_row - 1) * prow
         at_ports, at_xfs = [], []
         for h in range(2):
             lanes = slice(h * HALF, (h + 1) * HALF)
             for dirn in range(2):
                 arrived(rs_recv.at[t, dirn, 3, h], rs_rsem.at[t, dirn, 3, h])
             left, right = rs_recv.at[t, 0, 3, h], rs_recv.at[t, 1, 3, h]
-            at_ports.append(y[me, 0:ports, lanes] + left[0:ports].astype(F32) + right[0:ports].astype(F32))
-            at_xfs.append(y[me, ports : ports + xfs, lanes] + both(left[ports:prow]) + both(right[ports:prow]))
+            at_ports.append(y[own : own + ports, lanes] + left[0:ports].astype(F32) + right[0:ports].astype(F32))
+            at_xfs.append(y[own + ports : own + ports + xfs, lanes] + both(left[ports:prow]) + both(right[ports:prow]))
         return at_ports, at_xfs
 
     s3_cut = other // 2
@@ -342,7 +364,8 @@
         zl[c, :, ports:] = dot_t(zm[:, pl.ds(pl.multiple_of(c * rows, rows), rows)], hot).astype(BF)
         return carry
 
-    products(me)
+    products(n_row - 1)
+    static_products(n_row - 1)
     vacc[...] = jnp.zeros_like(vacc)
     add_static(me)
     for d in range(1, n_row):
@@ -351,21 +374,25 @@
 
     for t in range(last):
 
-        def ready(d, t=t):
-            if t == 0 and d == n_hop:
+        def ready(stage, t=t):
+            if t:
+                if stage == 0:
+                    add_dynamic(t, 0, 3)
+                elif stage == 1:
+                    add_dynamic(t, 3, n_row)
+                return
+            if stage > 0:
+                for i in (0,) if stage == 1 else (2 * stage - 3, 2 * stage - 2):
+                    static_products(i)
+            if stage in (0, 2):
                 for _ in range(2):
                     next_ports()
-            if t == 0 and d == n_hop - 2:
-                for _ in range(2):
-                    next_ports()
-            for e in (d, n_row - d) if 0 < d < n_hop else (d,):
+            for i in (0,) if stage == 0 else (2 * stage - 1, 2 * stage) if stage < 4 else ():
+                e = places[i]
                 r = row_of(e)
-                if t:
-                    add_dynamic(t, r)
-                elif e:
-                    arrived(zc.at[r, pl.ds(0, ports)], z_recv.at[0, n_row - e])
-                    arrived(zcx.at[r], z_recv.at[1, n_row - e])
-                    products(r)
+                arrived(zc.at[r, pl.ds(0, ports)], z_recv.at[0, n_row - e])
+                arrived(zcx.at[r], z_recv.at[1, n_row - e])
+                products(i)
 
         at_ports, at_xfs = reduce_scatter(t, ready)
         xv = jnp.concatenate(at_xfs, axis=1)
@@ -442,12 +469,21 @@
     add_last(row_of(3))
     for p in range(2):
         d3_wait(p, 3, p)
-    add_last(row_of(n_hop))
-    out_copy = pltpu.make_async_copy(vacc.at[pl.ds(0, rows)], vout, load_sem.at[0])
-    out_copy.start()
-    flux0[...] = flux + 0.5 * (vacc[rows : rows + xfs] + xprev)
-    flux_copy = pltpu.make_async_copy(flux0, fout, load_sem.at[1])
-    flux_copy.start()
+    far_row = row_of(n_hop)
+    piece = rows // 2
+    outs = []
+    for i in (1, 0):
+        n = piece + xr2 * i
+        vacc[i * piece : i * piece + n] += dot(zl[far_row, i * piece : i * piece + n], d3[far_row])
+        at = pl.ds(i * piece, piece)
+        cp = pltpu.make_async_copy(vacc.at[at], vout.at[at], load_sem.at[i])
+        cp.start()
+        outs.append(cp)
+        if i:
+            flux0[...] = flux + 0.5 * (vacc[rows : rows + xfs] + xprev)
+            cp = pltpu.make_async_copy(flux0, fout, in_sem.at[0])
+            cp.start()
+            outs.append(cp)
 
     for cp in z_copies + port_copies[-3:] + sends:
         cp.wait_send()
@@ -457,8 +493,8 @@
     for t in range(last):
         total = pl.ds(0, (n_sub - 1) * 2 * SLOTS)
         pltpu.make_async_copy(xs.at[t, total], xr.at[t, total], x_ssem.at[t]).wait()
-    out_copy.wait()
-    flux_copy.wait()
+    for cp in outs:
+        cp.wait()
 
 
 def hand_over(acc, flux_in, vout, fout):
@@ -504,9 +540,9 @@
             pltpu.VMEM((n_row, xr2, rows // 2), BF),
             pltpu.VMEM((n_row, prow, rows), BF),
             pltpu.VMEM((n_row, xr2, rows // 2), BF),
-            pltpu.VMEM((n_row, prow, ports + 128), BF),
-            pltpu.VMEM((last - 1, n_row, prow, scen), F32),
-            pltpu.VMEM((n_row, prow, scen), F32),
+            pltpu.VMEM((n_row * prow, ports + 128), BF),
+            pltpu.VMEM((last - 1, n_row * prow, scen), F32),
+            pltpu.VMEM((n_row * prow, scen), F32),
             pltpu.VMEM((last, 2, 4, 2, prow, HALF), BF),
             pltpu.VMEM((last, 2, 4, 2, prow, HALF), BF),
             pltpu.VMEM((last, n_slot, HALF), BF),

time: 104 us -> 104 us (level)
  no operation moved by 1% of the time
where the time goes in v4:
time: 104 us; the launch traced here: 103 us
  Pallas kernels  103 us (99%)
    pallas_call x1, Pallas kernels, body(): pl.pallas_call(functools.partial(kernel, n_sub, n_row, rows, ports, xfs,...  101 us

profile of v4, /device:TPU:2, one launch (start us, length us, event | category | flops | bytes accessed | tf_op | source)
XLA Modules:
  0.0 103.2 jit_solution(5985333880048358715)
XLA Ops:
  0.6 100.6 %grid_steps.1 = (f32[512,256]{1,0:T(8,128)}, f32[8,256]{1,0:T(8,128)}) custom-call(bf16[4,512,256]{2,1,0:T(8,128)(2,1)} %bitcast.12, bf16[512,4096]{1,0:T(8,128)(2,1)} %bitcast.11, s32[2,16]{1,0:T(2,128)} %bitcast.16, s32[2,128]{1,0:T(2,128)} %bitcast.17, s32[1,128]{1,0:T(1,128)} %delay_in.1, s32[1,8]{1,0:T(1,128)} %xf_in.1, bf16[2,128,256]{2,1,0:T(8,128)(2,1)} %bitcast.13, ...), custom_call_target="tpu_custom_call" | custom-call | tf_op jit(solution)/shard_map/grid_steps/pallas_call | solution.py:520
  101.3 1.9 %hand_over.1 = (f32[512,256]{1,0:T(8,128)}, f32[8,256]{1,0:T(8,128)}) custom-call(f32[512,256]{1,0:T(8,128)} %get-tuple-element.6.acc, f32[8,256]{1,0:T(8,128)} %get-tuple-element.7.flux_in), custom_call_target="tpu_custom_call" | custom-call | tf_op jit(solution)/shard_map/hand_over/pallas_call | solution.py:595
